TPU v7x, 128 devices: a whole 4x4x4 slice. The times are simulated.
128 devices in a mesh: ctx: 32 (over y, z, core), head: 4 (over x).
Axes of the slice: x: 4, y: 4, z: 4, core: 2. Of those that a mesh axis runs over, the one named last changes fastest.
Arguments:
- hidden: bfloat16 [4096, 2304], P('ctx'), may hold values from -6 to 6
- proj_weight: bfloat16 [3, 2304, 4096], P(None, None, 'head'), may hold values from -0.125 to 0.125
- conv_weight: float32 [3, 4, 4096], P(None, None, 'head'), may hold values from -3 to 3
- log_decay: float32 [4096, 4096], P('ctx', 'head'), may hold values from -1 to 0, as said below
- write_beta: float32 [4096, 32], P('ctx', 'head'), may hold values from 0 to 1, as said below
- saved_state: float32 [32, 32, 128, 128], P('ctx', 'head'), may hold values from -3 to 3
- output_grad: bfloat16 [4096, 4096], P('ctx', 'head'), may hold values from -6 to 6
- doc_lengths: int32 [8], replicated, may hold values from 1 to 2048, 4096 in all
Outputs:
- weight_grads: float32 [2304, 3, 4096], P('ctx', None, 'head')
- input_grad: bfloat16 [4096, 2304], P(('ctx', 'head'))
- decay_grad: float32 [4096, 4096], P('ctx', 'head')
Inputs may be any that keep to these rules, and one draw needn't show every extreme that they name: `doc_lengths`: the 8 lengths sum to 4096, and the longest is exactly half of 4096. `log_decay`: every entry is negative. `write_beta`: every entry is positive and below one.
All inputs are finite; a program needn't handle non-finite values.
Results may differ from a plain program's by a relative error of at most 0.02.
Values may be sent and summed in bfloat16 or wider, within the bound.
A program may use at most 192 MiB of HBM per device.

v0:
```python
import jax
import jax.numpy as jnp
from jax import lax
from jax.sharding import PartitionSpec as P

SPAN = 64


EPSILON = 1e-06
TOP_PRECISION = lax.Precision.HIGHEST


def passed_along(block, axis, distance):
    devices = range(lax.axis_size(axis))
    route = [(i - distance, i) for i in devices if i - distance in devices]
    return lax.ppermute(block, axis, route)


def doc_starts(doc_lengths, positions):
    starts = jnp.cumsum(doc_lengths, dtype=jnp.int32) - doc_lengths
    before = starts[None, :] <= positions[:, None]
    return jnp.max(jnp.where(before, starts[None, :], 0), axis=1)


def features(extended, conv_weight, seg_start, positions, head_count):
    tap_count = conv_weight.shape[1]
    tok_rows = positions.shape[0]
    mixed = jnp.zeros((extended.shape[0], tok_rows, extended.shape[2]), extended.dtype)
    for offset in range(tap_count):
        first_row = tap_count - 1 - offset
        window = extended[:, first_row : first_row + tok_rows, :]
        usable = (positions - offset >= seg_start).astype(extended.dtype)
        mixed = mixed + window * conv_weight[:, offset, :][:, None, :] * usable[None, :, None]
    active = jax.nn.silu(mixed)
    shaped = active.reshape(3, tok_rows, head_count, -1)
    paired = shaped[:2]
    normed = paired / jnp.sqrt(jnp.sum(paired * paired, axis=-1, keepdims=True) + EPSILON)
    scaled = normed[0] * shaped.shape[-1] ** (-0.5)
    return (scaled, normed[1], shaped[2])


def span_step(incoming_state, queries, keys_in, values, log_decay, beta_rows, seg_start, positions):
    block_len = queries.shape[0]
    summed = jnp.cumsum(log_decay, axis=0)
    growth = jnp.exp(summed)
    shrink = jnp.exp(-summed)
    key_shifted_up = keys_in * growth
    key_minus = keys_in * shrink
    query_shifted_up = queries * growth
    leading_part = (seg_start < positions[0]).astype(growth.dtype)
    same_doc = (seg_start[:, None] == seg_start[None, :]).astype(growth.dtype)
    strict = jnp.tril(jnp.ones((block_len, block_len), growth.dtype), -1)
    inclusive = jnp.tril(jnp.ones((block_len, block_len), growth.dtype))
    coupling = (
        jnp.einsum("thk,shk->hts", key_shifted_up, key_minus, precision=TOP_PRECISION)
        * (same_doc * strict)[None]
    )
    reading = (
        jnp.einsum("thk,shk->hts", query_shifted_up, key_minus, precision=TOP_PRECISION)
        * (same_doc * inclusive)[None]
    )
    beta_heads = beta_rows.T
    system = jnp.eye(block_len, dtype=growth.dtype)[None] + beta_heads[:, :, None] * coupling
    recalled_value = (
        jnp.einsum("fju,jul->jfl", key_shifted_up, incoming_state, precision=TOP_PRECISION)
        * leading_part[None, :, None]
    )
    target = beta_heads[:, :, None] * (jnp.transpose(values, (1, 0, 2)) - recalled_value)
    written_value = lax.linalg.triangular_solve(
        system, target, left_side=True, lower=True, unit_diagonal=True
    )
    layer_output = (
        jnp.einsum("nwj,wjl->nwl", query_shifted_up, incoming_state, precision=TOP_PRECISION)
        * leading_part[:, None, None]
    )
    layer_output = layer_output + jnp.einsum(
        "hts,hsv->thv", reading, written_value, precision=TOP_PRECISION
    )
    final_decay = growth[-1]
    carried_over = key_minus * final_decay[None] * same_doc[-1][:, None, None]
    outgoing_state = incoming_state * (final_decay * leading_part[-1])[:, :, None]
    outgoing_state = outgoing_state + jnp.einsum(
        "pge,gpu->geu", carried_over, written_value, precision=TOP_PRECISION
    )
    return (layer_output, outgoing_state)


def recurrence(
    queries, keys_in, values, log_decay, beta_rows, incoming_state, seg_start, positions
):
    tok_rows, head_count, head_width = queries.shape
    blocks = tok_rows // SPAN

    def blocked(source):
        return source.reshape((blocks, SPAN) + source.shape[1:])

    decay_rows = log_decay.reshape(tok_rows, head_count, head_width)
    inputs = (
        blocked(queries),
        blocked(keys_in),
        blocked(values),
        blocked(decay_rows),
        blocked(beta_rows),
        blocked(seg_start),
        blocked(positions),
    )

    def recurrence_advance(state_now, block_in):
        layer_output, outgoing_state = span_step(state_now, *block_in)
        return (outgoing_state, layer_output)

    final_state, outputs = lax.scan(recurrence_advance, incoming_state, inputs)
    return (outputs.reshape(tok_rows, head_count, head_width), final_state)


def transition(keys_in, log_decay, beta_rows, seg_start, positions):
    tok_rows, head_count, head_width = keys_in.shape
    blocks = tok_rows // SPAN

    def blocked(source):
        return source.reshape((blocks, SPAN) + source.shape[1:])

    decay_rows = log_decay.reshape(tok_rows, head_count, head_width)
    inputs = (
        blocked(keys_in),
        blocked(decay_rows),
        blocked(beta_rows),
        blocked(seg_start),
        blocked(positions),
    )
    identity = jnp.broadcast_to(
        jnp.eye(head_width, dtype=jnp.float32), (head_count, head_width, head_width)
    )

    def transition_advance(product, block_in):
        key_block, decay_block, beta_block, seg_block, pos_block = block_in
        blank = jnp.zeros_like(key_block)
        moved = span_step(
            identity, blank, key_block, blank, decay_block, beta_block, seg_block, pos_block
        )[1]
        return (jnp.einsum("hij,hkj->hik", product, moved, precision=TOP_PRECISION), None)

    result, unused = lax.scan(transition_advance, identity, inputs)
    return result


def body(
    hidden, proj_weight, conv_weight, log_decay, write_beta, saved_state, output_grad, doc_lengths
):
    tok_rows = hidden.shape[0]
    head_count = write_beta.shape[1]
    head_width = saved_state.shape[-1]
    tap_count = conv_weight.shape[1]
    positions = lax.axis_index("ctx") * tok_rows + jnp.arange(tok_rows, dtype=jnp.int32)
    seg_start = doc_starts(doc_lengths, positions)
    projected = jnp.stack(
        [
            jnp.dot(hidden, proj_weight[matrix], preferred_element_type=jnp.float32)
            for matrix in range(3)
        ]
    ).astype(jnp.bfloat16)
    previous = passed_along(projected[:, tok_rows - tap_count + 1 :, :], "ctx", 1)
    extended = jnp.concatenate([previous, projected], axis=1).astype(jnp.float32)

    def shaped_features(source):
        return features(source, conv_weight, seg_start, positions, head_count)

    feature_set, feature_pull = jax.vjp(shaped_features, extended)
    start_state = saved_state[0]
    out_grad = output_grad.astype(jnp.float32).reshape(tok_rows, head_count, head_width)

    def local_chain(queries, keys_in, values, decay_rows, incoming_state):
        return recurrence(
            queries, keys_in, values, decay_rows, write_beta, incoming_state, seg_start, positions
        )

    unused, chain_pull = jax.vjp(
        local_chain, feature_set[0], feature_set[1], feature_set[2], log_decay, start_state
    )
    own_part = chain_pull((out_grad, jnp.zeros_like(start_state)))
    entry_grad = own_part[4]
    transposed = transition(feature_set[1], log_decay, write_beta, seg_start, positions)
    shard_count = lax.axis_size("ctx")

    def relay(step_num, pair):
        current, incoming = pair
        incoming = passed_along(current.astype(jnp.bfloat16), "ctx", -1).astype(current.dtype)
        current = (
            jnp.einsum("hij,hjv->hiv", transposed, incoming, precision=TOP_PRECISION) + entry_grad
        )
        return (current, incoming)

    unused_now, suffix_grad = lax.fori_loop(
        0, shard_count, relay, (entry_grad, jnp.zeros_like(entry_grad))
    )
    carried_part = chain_pull((jnp.zeros_like(out_grad), suffix_grad))
    summed_grads = [own_part[member] + carried_part[member] for member in range(4)]
    extended_grad = feature_pull((summed_grads[0], summed_grads[1], summed_grads[2]))[0]
    spill = passed_along(
        extended_grad[:, : tap_count - 1, :].astype(jnp.bfloat16), "ctx", -1
    ).astype(jnp.float32)
    inner = extended_grad[:, tap_count - 1 :, :]
    raw_grad = (inner + jnp.pad(spill, ((0, 0), (tok_rows - tap_count + 1, 0), (0, 0)))).astype(
        jnp.bfloat16
    )
    weight_grads = lax.psum_scatter(
        jnp.einsum("td,ptc->dpc", hidden, raw_grad, preferred_element_type=jnp.float32).astype(
            jnp.bfloat16
        ),
        "ctx",
        scatter_dimension=0,
        tiled=True,
    ).astype(jnp.float32)
    input_grad = lax.psum_scatter(
        jnp.einsum("ptc,pdc->td", raw_grad, proj_weight, preferred_element_type=jnp.float32).astype(
            jnp.bfloat16
        ),
        "head",
        scatter_dimension=0,
        tiled=True,
    )
    return (weight_grads, input_grad, summed_grads[3])


def solution(mesh):
    return jax.shard_map(
        body,
        mesh=mesh,
        in_specs=(
            P("ctx", None),
            P(None, None, "head"),
            P(None, None, "head"),
            P("ctx", "head"),
            P("ctx", "head"),
            P("ctx", "head", None, None),
            P("ctx", "head"),
            P(),
        ),
        out_specs=(P("ctx", None, "head"), P(("ctx", "head"), None), P("ctx", "head")),
        check_vma=False,
    )
```

profile of v0, /device:TPU:1, one launch (start us, length us, event | category | flops | bytes accessed | tf_op | source)
XLA Modules:
  0.0 1237.5 jit_solution(15648144855954020836)
XLA Ops:
  44.9 107.3 %while.127 = (s32[]{:T(128)}, f32[8,128,128]{1,2,0:T(8,128)}, f32[2,64,8,128]{3,2,1,0:T(8,128)}, s32[2,64]{1,0:T(2,128)S(1)}, s32[2,64]{1,0:T(2,128)}, /*index=5...) while((s32[]{:T(128)}, f32[8,128,128]{1,2,0:T(8,128)}, ...), condition=%wide.region_13.17_spmd.clone.clone, body=%wide.region_11.16_spmd.clone.clone.sunk | while | flops 508437760 | bytes 7882221 | solution.py:143
  53.7 40.1 %custom-call.45 = f32[8,1,64,64]{2,3,1,0:T(8,128)S(1)} custom-call(f32[8,1,64,64]{3,2,1,0:T(8,128)} %fusion.524), custom_call_target="InvertDiagBlocksLowerTriangular" | custom-call | tf_op jit(solution)/shard_map/while/body/eval_jaxpr/triangular_solve/custom-call.1 | solution.py:69
  107.3 40.1 %custom-call.45 = f32[8,1,64,64]{2,3,1,0:T(8,128)S(1)} custom-call(f32[8,1,64,64]{3,2,1,0:T(8,128)} %fusion.524), custom_call_target="InvertDiagBlocksLowerTriangular" | custom-call | tf_op jit(solution)/shard_map/while/body/eval_jaxpr/triangular_solve/custom-call.1 | solution.py:69
  156.3 141.5 %while.126 = (s32[]{:T(128)}, f32[8,128,128]{2,1,0:T(8,128)S(1)}, f32[2,64,8,128]{3,1,2,0:T(8,128)}, f32[2,64,8,128]{3,1,2,0:T(8,128)}, f32[2,64,8,128]{3,1,2,0:...) while((s32[]{:T(128)}, f32[8,128,128]{2,1,0:T(8,128)S(1)}, ...), condition=%wide.region_5.7_spmd.clone.clone, body=%wide.region_3.6_spmd.clone.clone.sunk | while | flops 358042176 | bytes 44277624 | solution.py:112
  179.2 40.7 %custom-call.44 = f32[8,1,64,64]{2,3,1,0:T(8,128)} custom-call(f32[8,1,64,64]{3,2,1,0:T(8,128)} %add_bitcast_fusion.2), custom_call_target="InvertDiagBlocksLowerTriangular" | custom-call | tf_op jit(solution)/shard_map/jvp()/while/body/eval_jaxpr/triangular_solve/custom-call.1 | solution.py:69
  249.9 40.7 %custom-call.44 = f32[8,1,64,64]{2,3,1,0:T(8,128)} custom-call(f32[8,1,64,64]{3,2,1,0:T(8,128)} %add_bitcast_fusion.2), custom_call_target="InvertDiagBlocksLowerTriangular" | custom-call | tf_op jit(solution)/shard_map/jvp()/while/body/eval_jaxpr/triangular_solve/custom-call.1 | solution.py:69
  301.1 134.2 %while.128 = (s32[]{:T(128)}, f32[8,128,128]{2,1,0:T(8,128)S(1)}, f32[2,64,8,128]{3,2,1,0:T(8,128)}, f32[2,64,8,128]{3,2,1,0:T(8,128)}, f32[2,64,8,128]{3,2,1,0:...) while((s32[]{:T(128)}, f32[8,128,128]{2,1,0:T(8,128)S(1)}, ...), condition=%wide.region_10.14_spmd.clone, body=%wide.region_6.13_spmd.clone.sunk | while | flops 1039249472 | bytes 54000484 | solution.py:112
  312.4 40.0 %custom-call.46 = f32[8,1,64,64]{2,3,1,0:T(8,128)S(1)} custom-call(f32[8,1,64,64]{3,2,1,0:T(8,128)} %fusion.556), custom_call_target="InvertDiagBlocksLowerTriangular" | custom-call | tf_op jit(solution)/shard_map/transpose(jvp())/while/body/eval_jaxpr/triangular_solve/custom-call.0 | solution.py:69
  379.4 40.0 %custom-call.46 = f32[8,1,64,64]{2,3,1,0:T(8,128)S(1)} custom-call(f32[8,1,64,64]{3,2,1,0:T(8,128)} %fusion.556), custom_call_target="InvertDiagBlocksLowerTriangular" | custom-call | tf_op jit(solution)/shard_map/transpose(jvp())/while/body/eval_jaxpr/triangular_solve/custom-call.0 | solution.py:69
  436.1 387.4 %while.124 = (s32[]{:T(128)}, bf16[8,128,128]{2,1,0:T(8,128)(2,1)}, f32[8,128,128]{2,1,0:T(8,128)}, f32[8,128,128]{2,1,0:T(8,128)}, f32[8,128,128]{2,1,0:T(8,128)S(1)}, /*index=5*/s32[]{:T(128)}) while((s32[]{:T(128)}, bf16[8,128,128]{2,1,0:T(8,128)(2,1)}, f32[8,128,128]{2,1,0:T(8,128)}, f32[8,128,128]{2,1,0:T(8,128)}, ...), condition=%wide.region_15.19_spmd, body=%wide.region_14.18_spmd.sunk | while | flops 201719808 | bytes 3407981 | solution.py:193
  604.7 8.1 collective-permute-done
  630.6 8.1 collective-permute-done
  656.6 8.1 collective-permute-done
  682.6 8.1 collective-permute-done
  708.5 8.1 collective-permute-done
  734.5 8.1 collective-permute-done
  760.4 8.1 collective-permute-done
  812.4 8.1 collective-permute-done
  826.8 132.9 %while.125 = (s32[]{:T(128)}, f32[8,128,128]{2,1,0:T(8,128)S(1)}, f32[2,64,8,128]{3,2,1,0:T(8,128)}, f32[2,64,8,128]{3,2,1,0:T(8,128)}, f32[2,64,8,128]{3,2,1,0:...) while((s32[]{:T(128)}, f32[8,128,128]{2,1,0:T(8,128)S(1)}, ...), condition=%wide.region_20.24_spmd.clone, body=%wide.region_16.23_spmd.clone.sunk | while | flops 1038594176 | bytes 50329836 | solution.py:112
  838.2 40.0 %custom-call.43 = f32[8,1,64,64]{2,3,1,0:T(8,128)S(1)} custom-call(f32[8,1,64,64]{3,2,1,0:T(8,128)} %fusion.481), custom_call_target="InvertDiagBlocksLowerTriangular" | custom-call | tf_op jit(solution)/shard_map/transpose(jvp())/while/body/eval_jaxpr/triangular_solve/custom-call.0 | solution.py:69
  904.5 40.0 %custom-call.43 = f32[8,1,64,64]{2,3,1,0:T(8,128)S(1)} custom-call(f32[8,1,64,64]{3,2,1,0:T(8,128)} %fusion.481), custom_call_target="InvertDiagBlocksLowerTriangular" | custom-call | tf_op jit(solution)/shard_map/transpose(jvp())/while/body/eval_jaxpr/triangular_solve/custom-call.0 | solution.py:69
  984.6 30.8 %copy.369 = bf16[2304,3,1024]{2,1,0:T(4,128)(2,1)} copy(bf16[2304,3,1024]{0,2,1:T(8,128)(2,1)} %convert_bitcast_fusion.1) | data formatting | bytes 28311552 | tf_op jit(solution)/shard_map/convert_element_type | solution.py:207
  1015.5 10.7 fusion.248
  1028.4 198.8 %all-reduce.14.cloned.1.call-done = bf16[2304,3,1024]{2,1,0:T(4,128)(2,1)} async-done(((bf16[2304,3,1024]{2,1,0:T(4,128)(2,1)}), bf16[2304,3,1024]{2,1,0:T(4,128)(2,1)}) %all-reduce.14.cloned.1.call-update) | async-done | bytes 14155792
  (855 shorter events, 590.0 us)
Async XLA Ops:
  8.0 1219.2 %all-reduce.14.cloned.1.call-start = ((), (), s32[]{:S(2)}) async-start(), calls=%async_computation.2 | async-start | bytes 37748736
  19.3 13.8 %collective-permute-start.1 = (bf16[3,3,1024]{2,1,0:T(4,128)(2,1)}, bf16[3,3,1024]{2,1,0:T(4,128)(2,1)}, u32[]{:S(2)}, u32[]{:S(2)}) collective-permute-start(bf16[3,3,1024]{2,1,0:T(4,128)(2,1)} %pad_maximum_fusion), channel_id=1, source_target_pairs={{0,4},{4,8},{8,12},{12,16},{16,20},{20,24},{24,28},{28,32},{32,36}... | collective-permute-start | bytes 55304 | tf_op jit(solution)/shard_map/ppermute | solution.py:16
  436.1 7.9 collective-permute-start
  479.6 7.9 collective-permute-start
  577.4 9.4 collective-permute-start
  589.8 10.0 collective-permute-start
  602.8 10.0 collective-permute-start
  615.7 10.0 collective-permute-start
  628.7 10.0 collective-permute-start
  641.7 10.0 collective-permute-start
  654.7 10.0 collective-permute-start
  667.7 10.0 collective-permute-start
  680.6 10.0 collective-permute-start
  693.6 10.0 collective-permute-start
  706.6 10.0 collective-permute-start
  719.6 10.0 collective-permute-start
  732.6 10.0 collective-permute-start
  745.5 10.0 collective-permute-start
  758.5 10.0 collective-permute-start
  771.5 10.0 collective-permute-start
  784.5 10.0 collective-permute-start
  797.5 10.0 collective-permute-start
  810.5 10.0 collective-permute-start
  1015.5 214.4 %reduce-scatter.2.cloned.1.call-start = ((), (), s32[]{:S(2)}) async-start(), calls=%async_computation.1 | async-start | bytes 737280 | tf_op jit(solution)/shard_map/reduce_scatter | solution.py:214
  (208 other events, 824.9 us)
Sparse Core Ops, SparseCore 0:
  1015.5 211.6 all-reduce.13
Sparse Core Ops, SparseCore 1:
  1026.3 47.9 reduce-scatter.1
where the time goes:
time: 1250 us; the launch traced here: 1240 us
  waiting for transfers between devices  435 us (35%)
  other arithmetic  410 us (33%)
  matrix products  174 us (14%)
  local copies, waits for them, and re-layouts  129 us (10%)
  starting transfers between devices  68 us (5%)
  between operations  17.2 us (1%)
    another operation x36, other arithmetic, span_step(): lax.linalg.triangular_solve(system, target, left_side=True, lower=True, u...  332 us
    ppermute x34, waiting for transfers between devices, passed_along(): return lax.ppermute(block, axis, route)  236 us
    unnamed x3, waiting for transfers between devices  199 us
    dot_general x32, matrix products, relay(): jnp.einsum('hij,hjv->hiv', transposed, incoming, precision=TOP_PRECISION)  68.3 us
    ppermute x34, starting transfers between devices, passed_along(): return lax.ppermute(block, axis, route)  67.9 us
    convert_element_type x1, local copies, waits for them, and re-layouts, body(): jnp.einsum('td,ptc->dpc', hidden, raw_grad, preferred_element_type=jnp.fl...  30.8 us
    convert_element_type x32, other arithmetic, relay(): passed_along(current.astype(jnp.bfloat16), 'ctx', -1).astype(current.dtype)  27.1 us
  transfers between devices with their start and end apart: 36, of which 34 were waited for; matrix products, arithmetic and copies ran while one was open for 2% of the time, Pallas kernels for 0%

commit v1 on v0

v1 whole, which is shorter than its diff:
```python
import functools

import jax
import jax.numpy as jnp
from jax import lax
from jax.experimental import pallas as pl
from jax.experimental.pallas import tpu as pltpu
from jax.sharding import PartitionSpec as P

MESH = pl.DeviceIdType.MESH
F32, BF16 = jnp.float32, jnp.bfloat16
EPSILON = 1e-06
HEADS, TOK, DK, D = 8, 128, 128, 2304
ROW, ROWS = 8, 4
SLAB, PADDED = 72, 80
HALO = 16
NN, NT, TN = (((1,), (0,)), ((), ())), (((1,), (1,)), ((), ())), (((0,), (0,)), ((), ()))


def dot1(a, b, form=NN):
    return lax.dot_general(a.astype(BF16), b.astype(BF16), form, preferred_element_type=F32)


def split(a):
    high = a.astype(BF16)
    return high, (a - high.astype(F32)).astype(BF16)


def dot3(a, b, form=NN):
    (ah, al), (bh, bl) = split(a), split(b)
    (la,), (lb,) = form[0]
    left = jnp.concatenate([ah, al, ah], axis=la)
    right = jnp.concatenate([bh, bh, bl], axis=lb)
    return lax.dot_general(left, right, form, preferred_element_type=F32)


def dot_exact_left(a, b):
    bh, bl = split(b)
    return lax.dot_general(
        jnp.concatenate([a, a], axis=1), jnp.concatenate([bh, bl], axis=0), NN, preferred_element_type=F32
    )


def iota(dim):
    return lax.broadcasted_iota(jnp.int32, (TOK, TOK), dim)


def me():
    return lax.axis_index("ctx"), lax.axis_index("head")


def chain_kernel(
    doc_ref, hid_ref, w_ref, conv_ref, ld_ref, beta_ref, s0_ref, og_ref,
    raw_ref, dld_ref, ht_ref,
    xext, wbuf, pe, ht_t, ht_send, ht_recv, norm, val, inv, dsil, masks, bet,
    grow, shrink, tinv, read, mb, rx, pc, tot, ry, ds, rd, uu, wl, tk, dkm, gg,
    tail, spill, spill_in,
    w_sem, x_sem, halo_sem, ht_ssem, ht_rsem, mb_ssem, mb_rsem, ry_ssem, ry_rsem, ds_ssem, ds_rsem, sp_sem,
):
    ctx, head = me()
    row, col = ctx // ROW, lax.rem(ctx, ROW)
    after, before = lax.rem(ctx + 1, ROW * ROWS), lax.rem(ctx + ROW * ROWS - 1, ROW * ROWS)

    def w_copy(group):
        at = pl.ds(pl.multiple_of(group * 256, 256), 256)
        return pltpu.make_async_copy(w_ref.at[:, :, at], wbuf.at[:, :, at], w_sem.at[group])

    for group in range(4):
        w_copy(group).start()
    x_copy = pltpu.make_async_copy(hid_ref, xext.at[pl.ds(HALO, TOK)], x_sem)
    x_copy.start()

    barrier = pltpu.get_barrier_semaphore()
    for step in range(1, ROW):
        mate = row * ROW + lax.rem(col + step, ROW)
        pl.semaphore_signal(barrier, inc=1, device_id=(mate, head), device_id_type=MESH)
    for step in range(1, ROWS):
        mate = lax.rem(row + step, ROWS) * ROW + col
        pl.semaphore_signal(barrier, inc=1, device_id=(mate, head), device_id_type=MESH)
    for mate in (after, before):
        pl.semaphore_signal(barrier, inc=1, device_id=(mate, head), device_id_type=MESH)

    t, s = iota(0), iota(1)
    first = ctx * TOK
    seg_t, seg_s = jnp.zeros_like(t), jnp.zeros_like(s)
    seg_last, start = jnp.int32(0), jnp.int32(0)
    for doc in range(8):
        seg_t = jnp.where(t + first >= start, jnp.maximum(seg_t, start), seg_t)
        seg_s = jnp.where(s + first >= start, jnp.maximum(seg_s, start), seg_s)
        seg_last = jnp.where(first + TOK - 1 >= start, jnp.maximum(seg_last, start), seg_last)
        start = start + doc_ref[doc]
    same = seg_t == seg_s
    masks[0] = jnp.where(same & (t > s), 1.0, 0.0)
    masks[1] = jnp.where(same & (t >= s), 1.0, 0.0)
    masks[2] = jnp.where(seg_t < first, 1.0, 0.0)
    masks[3] = jnp.where(seg_t == seg_last, 1.0, 0.0)
    for offset in range(1, 4):
        masks[3 + offset] = jnp.where(t + first - offset >= seg_t, 1.0, 0.0)
    lead_last = jnp.where(seg_last < first, 1.0, 0.0)
    for h in range(HEADS):
        bet[h] = jnp.broadcast_to(beta_ref[:, h : h + 1], (TOK, TOK))

    pl.semaphore_wait(barrier, ROW - 1 + ROWS - 1 + 2)

    halo = pltpu.make_async_remote_copy(
        src_ref=hid_ref.at[pl.ds(TOK - HALO, HALO)], dst_ref=xext.at[pl.ds(0, HALO)],
        send_sem=halo_sem.at[0], recv_sem=halo_sem.at[1], device_id=(after, head), device_id_type=MESH,
    )
    halo.start()

    for tile in range(D // 128):
        ht_t[tile * 128 : tile * 128 + 128] = hid_ref[:, tile * 128 : tile * 128 + 128].astype(F32).T
    ht_t[D : D + 8] = jnp.zeros((8, TOK), F32)
    for owner in range(ROW):
        for part in range(ROWS):
            base = (part * ROW + owner) * SLAB
            ht_send[owner, part * PADDED : part * PADDED + PADDED] = ht_t[base : base + PADDED].astype(BF16)

    def ht_copy(step):
        mate = lax.rem(col + step, ROW)
        return pltpu.make_async_remote_copy(
            src_ref=ht_send.at[mate], dst_ref=ht_recv.at[:, pl.ds(pl.multiple_of(col * TOK, TOK), TOK)],
            send_sem=ht_ssem.at[step], recv_sem=ht_rsem.at[step],
            device_id=(row * ROW + mate, head), device_id_type=MESH,
        )

    for step in range(1, ROW):
        ht_copy(step).start()
    ht_recv[:, pl.ds(pl.multiple_of(col * TOK, TOK), TOK)] = ht_send[col]

    x_copy.wait()
    halo.wait()

    def project(group, carry):
        w_copy(group).wait()
        wide = pl.ds(pl.multiple_of(group * 256, 256), 256)
        for p in range(3):
            made = jnp.dot(xext[...], wbuf[p, :, wide], preferred_element_type=F32)
            pe[p, :, wide] = made.astype(BF16).astype(F32)
        for half in range(2):
            h = group * 2 + half
            lanes = pl.ds(pl.multiple_of(h * DK, DK), DK)
            for p in range(3):
                mixed = pe[p, pl.ds(HALO, TOK), lanes] * conv_ref[p, 0:1, lanes]
                for offset in range(1, 4):
                    tap = pe[p, pl.ds(HALO - offset, TOK), lanes] * conv_ref[p, offset : offset + 1, lanes]
                    mixed = mixed + tap * masks[3 + offset]
                gate = 1.0 / (1.0 + jnp.exp(-mixed))
                active = mixed * gate
                dsil[p, h] = gate * (1.0 + mixed * (1.0 - gate))
                if p == 2:
                    val[h] = active
                else:
                    scale = lax.rsqrt(jnp.sum(active * active, axis=1, keepdims=True) + EPSILON)
                    norm[p, h] = active * scale
                    inv[p, h] = jnp.broadcast_to(scale, (TOK, DK))
        return carry

    lax.fori_loop(0, 4, project, 0)

    def mb_copy(h):
        return pltpu.make_async_remote_copy(
            src_ref=mb.at[h], dst_ref=rx.at[col], send_sem=mb_ssem.at[h], recv_sem=mb_rsem.at[col],
            device_id=(row * ROW + h, head), device_id_type=MESH,
        )

    batch = 4

    def transition(step, carry):
        heads = [step * batch + k for k in range(batch)]
        lanes = [pl.ds(pl.multiple_of(h * DK, DK), DK) for h in heads]
        below = (iota(0) >= iota(1)).astype(F32).astype(BF16)
        summed = [dot_exact_left(below, ld_ref[:, lane]) for lane in lanes]
        mids = [x[63:64] for x in summed]
        ups = [jnp.exp(x - mid) for x, mid in zip(summed, mids)]
        downs = [jnp.exp(mid - x) for x, mid in zip(summed, mids)]
        for h, up, down, mid in zip(heads, ups, downs, mids):
            grow[h], shrink[h] = up, down
        keys = [norm[1, h] for h in heads]
        queries = [norm[0, h] * DK ** (-0.5) for h in heads]
        low = [k * x for k, x in zip(keys, downs)]
        high = [jnp.concatenate([k * x, q * x], axis=0) for k, q, x in zip(keys, queries, ups)]
        both = [dot3(a, b, NT) for a, b in zip(high, low)]
        ns = [jnp.where(masks[0] > 0, x[:TOK], 0.0) * bet[h] for x, h in zip(both, heads)]
        rs = [jnp.where(masks[1] > 0, x[TOK:], 0.0) for x in both]
        apart = iota(0) ^ iota(1)
        eye = (apart == 0).astype(F32)
        solved = [eye - jnp.where(apart == 1, n, 0.0) for n in ns]
        for level in range(1, 7):
            edge = [jnp.where((apart >> level) == 1, n, 0.0) for n in ns]
            edge = [dot3(e, x) for e, x in zip(edge, solved)]
            solved = [x - dot3(x, e) for e, x in zip(edge, solved)]
        for h, x, r in zip(heads, solved, rs):
            tinv[h], read[h] = x, r.astype(BF16)
        lead = masks[2]
        firsts = [jnp.exp(mid) for mid in mids]
        ups0 = [x * e * lead for x, e in zip(ups, firsts)]
        ws = [dot1(x, bet[h] * k * up) for x, h, k, up in zip(solved, heads, keys, ups0)]
        xs = [q * up - dot1(r, w) for q, up, r, w in zip(queries, ups0, rs, ws)]
        lasts = [jnp.exp(x[TOK - 1 :] - mid) for x, mid in zip(summed, mids)]
        ends = [x * last * masks[3] for x, last in zip(low, lasts)]
        for h, lane, w, x, end, last, e in zip(heads, lanes, ws, xs, ends, lasts, firsts):
            mb[h, :, 0:DK] = (eye * (last * e * lead_last) - dot1(w, end, TN)).astype(BF16)
            mb[h, :, DK:] = dot1(x, og_ref[:, lane], TN).astype(BF16)
            tk[h] = dot1(tinv[h], end, TN).astype(BF16)
        for h in heads:
            @pl.when(h != col)
            def _():
                mb_copy(h).start()
        return carry

    lax.fori_loop(0, HEADS // batch, transition, 0)
    rx[col] = mb[col]

    def shift_back(p, h, lane, grad_active):
        dmix = grad_active * dsil[p, h]
        t = iota(0)
        main = dmix * conv_ref[p, 0:1, lane]
        over = jnp.zeros((TOK, DK), F32)
        for offset in range(1, 4):
            part = dmix * masks[3 + offset] * conv_ref[p, offset : offset + 1, lane]
            part = pltpu.roll(part, TOK - offset, 0)
            inside = t < TOK - offset
            main = main + jnp.where(inside, part, 0.0)
            over = over + jnp.where(inside, 0.0, part)
        raw_ref[p, :, lane] = main.astype(BF16)
        tail[p, :, lane] = main[TOK - HALO :]
        spill[p, :, lane] = over[TOK - 8 :]

    def unnorm(p, h, grad):
        n = norm[p, h]
        return inv[p, h] * (grad - n * jnp.sum(n * grad, axis=1, keepdims=True))

    def local(step, carry):
        heads = [step * 2 + k for k in range(2)]
        for h in heads:
            lane = pl.ds(pl.multiple_of(h * DK, DK), DK)
            og = og_ref[:, lane]
            up, down = grow[h], shrink[h]
            first_e = jnp.exp(dot_exact_left((iota(1) < 64).astype(F32).astype(BF16), ld_ref[:, lane]))
            up0 = up * first_e * masks[2]
            q = norm[0, h] * DK ** (-0.5)
            k = norm[1, h]
            state = s0_ref[0, h].astype(BF16)
            recalled = dot1(k * up0, state)
            u = dot1(tinv[h], bet[h] * (val[h] - recalled)).astype(BF16)
            uu[h] = u
            dread = jnp.where(masks[1] > 0, dot1(og, u, NT), 0.0).astype(BF16)
            dq = dot1(dread, k * down) * up + dot1(og, state, NT) * up0
            dkm[h] = dot1(dread, q * up, TN)
            gg[h] = q * dq
            wl[h] = dot1(tinv[h], dot1(read[h], og, TN), TN)
            shift_back(0, h, lane, unnorm(0, h, dq * DK ** (-0.5)))
        return carry

    for j in range(ROW):
        @pl.when(j != col)
        def _():
            pltpu.make_async_remote_copy(
                src_ref=mb.at[j], dst_ref=rx.at[j], send_sem=mb_ssem.at[j], recv_sem=mb_rsem.at[j],
                device_id=(row * ROW + j, head), device_id_type=MESH,
            ).wait_recv()

    def compose(m, x, b):
        hi, lo = split(x)
        out = jnp.dot(m, jnp.concatenate([hi, lo], axis=1), preferred_element_type=F32)
        n = x.shape[1]
        return out[:, :n] + out[:, n:] + b

    x = rx[ROW - 1].astype(F32)
    pc[ROW - 2] = x
    zeros = jnp.zeros((DK, DK), F32)
    for j in range(ROW - 2, -1, -1):
        b = jnp.concatenate([zeros, rx[j, :, DK:].astype(F32)], axis=1)
        x = compose(rx[j, :, 0:DK], x, b)
        if j > 0:
            pc[j - 1] = x
    tot[...] = x.astype(BF16)

    def ry_copy(step):
        mate = lax.rem(row + step, ROWS) * ROW + col
        return pltpu.make_async_remote_copy(
            src_ref=tot, dst_ref=ry.at[ROWS - step], send_sem=ry_ssem.at[step], recv_sem=ry_rsem.at[step],
            device_id=(mate, head), device_id_type=MESH,
        )

    for step in range(1, ROWS):
        ry_copy(step).start()
    for step in range(1, ROWS):
        ry_copy(step).wait_recv()
    total = jnp.zeros((DK, DK), F32)
    for k in range(ROWS - 1, 0, -1):
        moved = compose(ry[k, :, 0:DK], total, ry[k, :, DK:].astype(F32))
        total = jnp.where(row + k < ROWS, moved, total)

    def ds_copy(j):
        return pltpu.make_async_remote_copy(
            src_ref=ds.at[j], dst_ref=rd.at[col], send_sem=ds_ssem.at[j], recv_sem=ds_rsem.at[col],
            device_id=(row * ROW + j, head), device_id_type=MESH,
        )

    total_b = total.astype(BF16)
    for j in range(ROW):
        if j == ROW - 1:
            ds[j] = total_b
        else:
            ds[j] = (dot1(pc[j, :, 0:DK], total_b) + pc[j, :, DK:]).astype(BF16)

        @pl.when(j != col)
        def _():
            ds_copy(j).start()

    rd[col] = ds[col]

    lax.fori_loop(0, HEADS // 2, local, 0)

    for j in range(ROW):
        @pl.when(j != col)
        def _():
            pltpu.make_async_remote_copy(
                src_ref=ds.at[j], dst_ref=rd.at[j], send_sem=ds_ssem.at[j], recv_sem=ds_rsem.at[j],
                device_id=(row * ROW + j, head), device_id_type=MESH,
            ).wait_recv()

    def carried(step, carry):
        heads = [step * 2 + k for k in range(2)]
        above = (iota(1) >= iota(0)).astype(F32).astype(BF16)
        ones = jnp.ones((8, DK), BF16)
        for h in heads:
            lane = pl.ds(pl.multiple_of(h * DK, DK), DK)
            up, down = grow[h], shrink[h]
            sums = dot_exact_left(
                jnp.where(iota(0) < 64, jnp.where(iota(1) < 64, 1.0, 0.0), jnp.where(iota(1) >= 64, 1.0, 0.0)).astype(BF16),
                ld_ref[:, lane],
            )
            first_e, last_e = jnp.exp(sums[0:1]), jnp.exp(sums[TOK - 1 :])
            lead = masks[2]
            k = norm[1, h]
            dnext = rd[h]
            state = s0_ref[0, h]
            u = uu[h]
            w = wl[h] + dot1(tk[h], dnext)
            bw = bet[h] * w
            da = jnp.where(masks[0] > 0, -dot1(bw, u, NT), 0.0).astype(BF16)
            dku = dot1(da, k * down) - dot1(bw * lead, state, NT) * first_e
            dkm_all = dkm[h] + dot1(da, k * up, TN)
            dend = dot1(u, dnext, NT) * last_e * masks[3]
            rising = dku * up
            ending = dend * down
            falling = dkm_all * down + ending
            dk = rising + falling
            dg = gg[h] + k * (rising - falling)
            crossed = state * dnext.astype(F32) * lead_last
            ch, cl = split(crossed)
            extra = dot1(ones, ch, NT) + dot1(ones, cl, NT)
            extra = extra[0:1] * first_e * last_e + jnp.sum(k * ending, axis=0, keepdims=True)
            dld_ref[:, lane] = dot_exact_left(above, dg) + extra
            shift_back(1, h, lane, unnorm(1, h, dk))
            shift_back(2, h, lane, bw)
        return carry

    lax.fori_loop(0, HEADS // 2, carried, 0)

    send = pltpu.make_async_remote_copy(
        src_ref=spill, dst_ref=spill_in, send_sem=sp_sem.at[0], recv_sem=sp_sem.at[1],
        device_id=(before, head), device_id_type=MESH,
    )
    send.start()
    for step in range(1, ROW):
        ht_copy(step).wait()
    ht_ref[...] = ht_recv[...]
    for step in range(1, ROWS):
        ry_copy(step).wait_send()
    for j in range(ROW):
        @pl.when(j != col)
        def _():
            mb_copy(j).wait_send()
            ds_copy(j).wait_send()
    send.wait()
    for p in range(3):
        low = tail[p, 8:16] + spill_in[p]
        raw_ref[p, TOK - HALO :, :] = jnp.concatenate([tail[p, 0:8], low], axis=0).astype(BF16)


def chain(doc_lengths, hidden, proj_weight, conv_weight, log_decay, write_beta, saved_state, output_grad):
    vm = pl.BlockSpec(memory_space=pltpu.VMEM)
    sq = (HEADS, TOK, DK)
    dma = pltpu.SemaphoreType.DMA
    return pl.pallas_call(
        chain_kernel,
        out_shape=(
            jax.ShapeDtypeStruct((3, TOK, HEADS * DK), BF16),
            jax.ShapeDtypeStruct((TOK, HEADS * DK), F32),
            jax.ShapeDtypeStruct((ROWS * PADDED, ROW * TOK), BF16),
        ),
        in_specs=[pl.BlockSpec(memory_space=pltpu.SMEM), vm, pl.BlockSpec(memory_space=pl.ANY), vm, vm, vm, vm, vm],
        out_specs=(vm, vm, vm),
        scratch_shapes=[
            pltpu.VMEM((HALO + TOK, D), BF16),
            pltpu.VMEM((3, D, HEADS * DK), BF16),
            pltpu.VMEM((3, HALO + TOK, HEADS * DK), F32),
            pltpu.VMEM((D + 8, TOK), F32),
            pltpu.VMEM((ROW, ROWS * PADDED, TOK), BF16),
            pltpu.VMEM((ROWS * PADDED, ROW * TOK), BF16),
            pltpu.VMEM((2,) + sq, F32),
            pltpu.VMEM(sq, F32),
            pltpu.VMEM((2,) + sq, F32),
            pltpu.VMEM((3,) + sq, F32),
            pltpu.VMEM((7, TOK, TOK), F32),
            pltpu.VMEM(sq, F32),
            pltpu.VMEM(sq, F32),
            pltpu.VMEM(sq, F32),
            pltpu.VMEM(sq, F32),
            pltpu.VMEM(sq, BF16),
            pltpu.VMEM((HEADS, DK, 2 * DK), BF16),
            pltpu.VMEM((ROW, DK, 2 * DK), BF16),
            pltpu.VMEM((ROW, DK, 2 * DK), F32),
            pltpu.VMEM((DK, 2 * DK), BF16),
            pltpu.VMEM((ROWS, DK, 2 * DK), BF16),
            pltpu.VMEM((ROW, DK, DK), BF16),
            pltpu.VMEM((HEADS, DK, DK), BF16),
            pltpu.VMEM(sq, BF16),
            pltpu.VMEM(sq, F32),
            pltpu.VMEM(sq, BF16),
            pltpu.VMEM(sq, F32),
            pltpu.VMEM(sq, F32),
            pltpu.VMEM((3, HALO, HEADS * DK), F32),
            pltpu.VMEM((3, 8, HEADS * DK), F32),
            pltpu.VMEM((3, 8, HEADS * DK), F32),
            dma((4,)), dma, dma((2,)), dma((ROW,)), dma((ROW,)), dma((ROW,)), dma((ROW,)),
            dma((ROWS,)), dma((ROWS,)), dma((ROW,)), dma((ROW,)), dma((2,)),
        ],
        compiler_params=pltpu.CompilerParams(
            collective_id=0, has_side_effects=True, vmem_limit_bytes=56 * 1024 * 1024
        ),
        cost_estimate=pl.CostEstimate(flops=4_000_000_000, bytes_accessed=18_000_000, transcendentals=1_000_000),
        name="chain",
    )(doc_lengths, hidden, proj_weight, conv_weight, log_decay, write_beta, saved_state, output_grad)


def grads_kernel(
    raw_ref, ht_ref, w_ref, wg_ref, ig_ref,
    wbuf, raws, part, psend, precv, ipart, isend, irecv,
    w_sem, own_sem, a_ssem, a_rsem, p_ssem, p_rsem, i_ssem, i_rsem,
):
    ctx, head = me()
    row, col = ctx // ROW, lax.rem(ctx, ROW)
    z, core = col // 2, lax.rem(col, 2)
    wide = HEADS * DK

    def device(zz, cc):
        return (row * ROW + lax.rem(zz, 4) * 2 + cc, head)

    def slot(zz, cc):
        return lax.rem(zz, 4) * 2 + cc

    up, down, twin = device(z + 1, core), device(z + 3, core), device(z, 1 - core)

    for p in range(3):
        pltpu.make_async_copy(w_ref.at[p], wbuf.at[p], w_sem.at[p]).start()

    barrier = pltpu.get_barrier_semaphore()
    for mate in (up, down, twin):
        pl.semaphore_signal(barrier, inc=1, device_id=mate, device_id_type=MESH)
    for step in range(1, 4):
        pl.semaphore_signal(
            barrier, inc=1, device_id=(lax.rem(row + step, ROWS) * ROW + col, head), device_id_type=MESH
        )
        pl.semaphore_signal(barrier, inc=1, device_id=(ctx, lax.rem(head + step, 4)), device_id_type=MESH)
    pl.semaphore_wait(barrier, 9)

    def rows_of(j):
        return pl.ds(pl.multiple_of(j * TOK, TOK), TOK)

    left, right = pl.ds(0, wide // 2), pl.ds(wide // 2, wide // 2)

    def gather(p, kind):
        mine = raw_ref.at[p]
        if kind == 0:
            src, dst, to = mine, raws.at[p, rows_of(slot(z, core))], up
        elif kind == 1:
            src, dst, to = mine, raws.at[p, rows_of(slot(z, core))], down
        elif kind == 2:
            src = dst = raws.at[p, rows_of(slot(z + 3, core)), left]
            to = up
        elif kind == 3:
            src = dst = raws.at[p, rows_of(slot(z + 1, core)), right]
            to = down
        elif kind == 4:
            src, dst, to = mine, raws.at[p, rows_of(slot(z, core))], twin
        else:
            src = dst = raws.at[p, rows_of(slot(z + (3, 1, 2)[kind - 5], core))]
            to = twin
        return pltpu.make_async_remote_copy(
            src_ref=src, dst_ref=dst, send_sem=a_ssem.at[p, kind], recv_sem=a_rsem.at[p, kind],
            device_id=to, device_id_type=MESH,
        )

    def own(p):
        return pltpu.make_async_copy(raw_ref.at[p], raws.at[p, rows_of(slot(z, core))], own_sem.at[p])

    for p in range(3):
        for kind in (0, 1, 4):
            gather(p, kind).start()
        own(p).start()

    def input_part(tile, carry):
        at = pl.ds(pl.multiple_of(tile * 256, 256), 256)
        total = jnp.zeros((TOK, 256), F32)
        for p in range(3):
            total = total + lax.dot_general(raw_ref[p], wbuf[p, at, :], NT, preferred_element_type=F32)
        ipart[:, at] = total
        return carry

    for p in range(3):
        pltpu.make_async_copy(w_ref.at[p], wbuf.at[p], w_sem.at[p]).wait()
    lax.fori_loop(0, D // 256, input_part, 0)
    isend[...] = ipart[...].astype(BF16)

    def input_copy(step):
        mate = lax.rem(head + step, 4)
        return pltpu.make_async_remote_copy(
            src_ref=isend.at[pl.ds(pl.multiple_of(mate * 32, 32), 32)], dst_ref=irecv.at[step],
            send_sem=i_ssem.at[step], recv_sem=i_rsem.at[step], device_id=(ctx, mate), device_id_type=MESH,
        )

    for step in range(1, 4):
        input_copy(step).start()

    def hand_on(p):
        gather(p, 0).wait_recv()
        gather(p, 2).start()
        gather(p, 5).start()
        gather(p, 1).wait_recv()
        gather(p, 3).start()
        gather(p, 6).start()

    def part_copy(p, step):
        mate = lax.rem(row + step, ROWS)
        return pltpu.make_async_remote_copy(
            src_ref=psend.at[p, pl.ds(pl.multiple_of(mate * PADDED, PADDED), PADDED)],
            dst_ref=precv.at[p, step], send_sem=p_ssem.at[p, step], recv_sem=p_rsem.at[p, step],
            device_id=(mate * ROW + col, head), device_id_type=MESH,
        )

    def finish(p):
        gather(p, 2).wait_recv()
        gather(p, 3).wait_recv()
        gather(p, 7).start()
        for kind in (4, 5, 6, 7):
            gather(p, kind).wait_recv()
        own(p).wait()

        def product(tile, carry):
            at = pl.ds(pl.multiple_of(tile * 256, 256), 256)
            made = jnp.dot(ht_ref[...], raws[p, :, at], preferred_element_type=F32)
            psend[p, :, at] = made.astype(BF16)
            part[:, at] = made
            return carry

        lax.fori_loop(0, wide // 256, product, 0)
        for step in range(1, ROWS):
            part_copy(p, step).start()
        wg_ref[p] = part[pl.ds(pl.multiple_of(row * PADDED, 8), SLAB), :]

    def receive(p):
        total = wg_ref[p]
        for step in range(1, ROWS):
            part_copy(p, step).wait_recv()
            total = total + precv[p, step].astype(F32)[:SLAB]
        wg_ref[p] = total

    hand_on(0)
    hand_on(1)
    finish(0)
    hand_on(2)
    finish(1)
    for step in range(1, 4):
        input_copy(step).wait_recv()
    total = ipart[pl.ds(pl.multiple_of(head * 32, 32), 32), :]
    for step in range(1, 4):
        total = total + irecv[step].astype(F32)
    ig_ref[...] = total.astype(BF16)
    finish(2)
    for p in range(3):
        receive(p)
    for p in range(3):
        for kind in range(8):
            gather(p, kind).wait_send()
        for step in range(1, ROWS):
            part_copy(p, step).wait_send()
    for step in range(1, 4):
        input_copy(step).wait_send()


def grads(raw, ht, proj_weight):
    vm = pl.BlockSpec(memory_space=pltpu.VMEM)
    dma = pltpu.SemaphoreType.DMA
    wide = HEADS * DK
    return pl.pallas_call(
        grads_kernel,
        out_shape=(
            jax.ShapeDtypeStruct((3, SLAB, wide), F32),
            jax.ShapeDtypeStruct((32, D), BF16),
        ),
        in_specs=[vm, vm, pl.BlockSpec(memory_space=pl.ANY)],
        out_specs=(vm, vm),
        scratch_shapes=[
            pltpu.VMEM((3, D, wide), BF16),
            pltpu.VMEM((3, ROW * TOK, wide), BF16),
            pltpu.VMEM((ROWS * PADDED, wide), F32),
            pltpu.VMEM((3, ROWS * PADDED, wide), BF16),
            pltpu.VMEM((3, ROWS, PADDED, wide), BF16),
            pltpu.VMEM((TOK, D), F32),
            pltpu.VMEM((TOK, D), BF16),
            pltpu.VMEM((4, 32, D), BF16),
            dma((3,)), dma((3,)), dma((3, 8)), dma((3, 8)), dma((3, ROWS)), dma((3, ROWS)), dma((4,)), dma((4,)),
        ],
        compiler_params=pltpu.CompilerParams(
            collective_id=1, has_side_effects=True, vmem_limit_bytes=56 * 1024 * 1024
        ),
        cost_estimate=pl.CostEstimate(flops=4_000_000_000, bytes_accessed=18_000_000, transcendentals=0),
        name="grads",
    )(raw, ht, proj_weight)


def body(hidden, proj_weight, conv_weight, log_decay, write_beta, saved_state, output_grad, doc_lengths):
    raw, decay_grad, ht = chain(
        doc_lengths, hidden, proj_weight, conv_weight, log_decay, write_beta, saved_state, output_grad
    )
    weight_grads, input_grad = grads(raw, ht, proj_weight)
    return (jnp.transpose(weight_grads, (1, 0, 2)), input_grad, decay_grad)


def solution(mesh):
    return jax.shard_map(
        body,
        mesh=mesh,
        in_specs=(
            P("ctx", None),
            P(None, None, "head"),
            P(None, None, "head"),
            P("ctx", "head"),
            P("ctx", "head"),
            P("ctx", "head", None, None),
            P("ctx", "head"),
            P(),
        ),
        out_specs=(P("ctx", None, "head"), P(("ctx", "head"), None), P("ctx", "head")),
        check_vma=False,
    )
```

time: 1250 us -> 113 us (0.09)
  waiting for transfers between devices: 435 us -> 0 us
  other arithmetic: 410 us -> 0 us
  matrix products: 174 us -> 0 us
  local copies, waits for them, and re-layouts: 129 us -> 5.97 us
  Pallas kernels: 0 us -> 106 us
  starting transfers between devices: 68 us -> 0 us
  between operations: 17.2 us -> 0.66 us
    another operation x61 -> x0, other arithmetic: 338 us -> none  [the longest x36 332 us: span_step(): lax.linalg.triangular_solve(system, target, left_side=True, lower=True, u...]
    ppermute x34 -> x0, waiting for transfers between devices: 236 us -> none  [passed_along(): return lax.ppermute(block, axis, route)]
    unnamed x3 -> x0, waiting for transfers between devices: 199 us -> none
    dot_general x105 -> x0, matrix products: 165 us -> none  [the longest x32 68.3 us: relay(): jnp.einsum('hij,hjv->hiv', transposed, incoming, precision=TOP_PRECISION)]
    pallas_call x0 -> x2, Pallas kernels: none -> 106 us  [the longest x1 56.1 us: grads(): pl.pallas_call(grads_kernel, out_shape=(jax.ShapeDtypeStruct((3, SLAB, wi...]
    ppermute x34 -> x0, starting transfers between devices: 67.9 us -> none  [passed_along(): return lax.ppermute(block, axis, route)]
    convert_element_type x2 -> x0, local copies, waits for them, and re-layouts: 31.5 us -> none  [the longest x1 30.8 us: body(): jnp.einsum('td,ptc->dpc', hidden, raw_grad, preferred_element_type=jnp.fl...]
    mul x31 -> x0, local copies, waits for them, and re-layouts: 31.3 us -> none  [the longest x8 9.98 us: span_step(): carried_over = key_minus * final_decay[None] * same_doc[-1][:, None, None]]
  transfers between devices with their start and end apart: 36 -> 0, of which waited for: 34 -> 0; matrix products, arithmetic and copies ran while one was open for 2% -> 0% of each run, Pallas kernels for 0% -> 0%
where the time goes in v1:
time: 113 us
  Pallas kernels  106 us (94%)
  local copies, waits for them, and re-layouts  5.97 us (5%)
    pallas_call x1, Pallas kernels, grads(): pl.pallas_call(grads_kernel, out_shape=(jax.ShapeDtypeStruct((3, SLAB, wi...  56.1 us
    pallas_call x1, Pallas kernels, chain(): pl.pallas_call(chain_kernel, out_shape=(jax.ShapeDtypeStruct((3, TOK, HEA...  50.1 us
    unnamed x6, local copies, waits for them, and re-layouts  5.97 us

profile of v1, /device:TPU:1, one launch (start us, length us, event | category | flops | bytes accessed | tf_op | source)
XLA Modules:
  0.0 112.8 jit_solution(16036652563245044382)
XLA Ops:
  0.6 1.4 %copy.11.beta_ref = f32[128,8]{1,0:T(8,128)} copy(f32[128,8]{0,1:T(8,128)} %param.12) | data formatting | bytes 8192 | tf_op args[4]
  2.0 50.1 %chain.1 = (bf16[3,128,1024]{2,1,0:T(8,128)(2,1)}, f32[128,1024]{1,0:T(8,128)}, bf16[320,1024]{1,0:T(8,128)(2,1)}) custom-call(s32[8]{0:T(128)} %doc_ref.1, bf16[128,2304]{1,0:T(8,128)(2,1)} %hid_ref.1, bf16[3,2304,1024]{2,1,0:T(8,128)(2,1)} %w_ref.3, f32[3,4,1024]{2,1,0:T(4,128)} %conv_ref.1, f32[128,1024]{1,0:T(8,128)} %ld_ref.1, f32[128,8]{1,0:T(8,128)} %copy.11.beta_ref, ...), custom_call_target="tpu_custom_call" | custom-call | flops 4000000000 | bytes 18000000 | tf_op jit(solution)/shard_map/chain/pallas_call | solution.py:389
  52.1 0.0 copy-start
  52.2 56.1 %grads.1 = (f32[3,72,1024]{2,1,0:T(8,128)}, bf16[32,2304]{1,0:T(8,128)(2,1)}) custom-call(bf16[3,128,1024]{2,1,0:T(8,128)(2,1)} %get-tuple-element.8.raw_ref, bf16[320,1024]{1,0:T(8,128)(2,1)} %get-tuple-element.9.ht_ref, bf16[3,2304,1024]{2,1,0:T(8,128)(2,1)} %w_ref.3), custom_call_target="tpu_custom_call" | custom-call | flops 4000000000 | bytes 18000000 | tf_op jit(solution)/shard_map/grads/pallas_call | solution.py:600
  108.3 2.2 %copy.15 = f32[72,3,1024]{2,0,1:T(8,128)} copy(f32[72,3,1024]{2,0,1:T(8,128)} %bitcast.1) | data formatting | bytes 1769472
  110.4 1.6 %copy.16 = bf16[32,2304]{1,0:T(8,128)(2,1)} copy(bf16[32,2304]{1,0:T(8,128)(2,1)} %get-tuple-element.17) | data formatting | bytes 294912
  112.0 0.0 copy-done
  112.0 0.8 copy.17
Async XLA Ops:
  52.1 59.9 %copy-start = (f32[128,1024]{1,0:T(8,128)S(1)}, f32[128,1024]{1,0:T(8,128)}, u32[]{:S(2)}) copy-start(f32[128,1024]{1,0:T(8,128)} %get-tuple-element.18) | copy-start | bytes 1572868

commit v2 on v1

v2 whole, which is shorter than its diff:
```python
import functools

import jax
import jax.numpy as jnp
from jax import lax
from jax.experimental import pallas as pl
from jax.experimental.pallas import tpu as pltpu
from jax.sharding import PartitionSpec as P

MESH = pl.DeviceIdType.MESH
F32, BF16 = jnp.float32, jnp.bfloat16
EPSILON = 1e-06
HEADS, TOK, DK, D = 8, 128, 128, 2304
ROW, ROWS = 8, 4
SLAB, PADDED = 72, 80
HALO = 16
NN, NT, TN = (((1,), (0,)), ((), ())), (((1,), (1,)), ((), ())), (((0,), (0,)), ((), ()))


def dot1(a, b, form=NN):
    return lax.dot_general(a.astype(BF16), b.astype(BF16), form, preferred_element_type=F32)


def split(a):
    high = a.astype(BF16)
    return high, (a - high.astype(F32)).astype(BF16)


def dot3(a, b, form=NN):
    (ah, al), (bh, bl) = split(a), split(b)
    (la,), (lb,) = form[0]
    left = jnp.concatenate([ah, al, ah], axis=la)
    right = jnp.concatenate([bh, bh, bl], axis=lb)
    return lax.dot_general(left, right, form, preferred_element_type=F32)


def dot_exact_left(a, b):
    bh, bl = split(b)
    return lax.dot_general(
        jnp.concatenate([a, a], axis=1), jnp.concatenate([bh, bl], axis=0), NN, preferred_element_type=F32
    )


def iota(dim):
    return lax.broadcasted_iota(jnp.int32, (TOK, TOK), dim)


def me():
    return lax.axis_index("ctx"), lax.axis_index("head")


UNITS = ((0, 0, 512, 0), (0, 512, 512, 1), (1, 0, 512, 0), (2, 0, 512, 1), (1, 512, 512, 0), (2, 512, 512, 1))


def chain_kernel(
    doc_ref, hid_ref, w_ref, conv_ref, ld_hbm, beta_ref, s0_hbm, og_hbm,
    wg_ref, ig_ref, dld_ref,
    ld_ref, s0_ref, og_ref, xext, wbuf, pe, ht_t, ht_send, ht_recv, norm, val, inv, dsil, masks, bet,
    grow, shrink, edges, tinv, read, mb, rx, pc, tot, ry, carry_in, ds, rd, uu, wl, tk, dkm, gg,
    tail, spill, spill_in, own, raws, part, psend, precv, ipart, isend, irecv,
    in_sem, w_sem, x_sem, halo_sem, ht_ssem, ht_rsem, mb_ssem, mb_rsem, ry_ssem, ry_rsem, ds_ssem, ds_rsem, sp_sem,
    a_ssem, a_rsem, p_ssem, p_rsem, i_ssem, i_rsem,
):
    ctx, head = me()
    row, col = ctx // ROW, lax.rem(ctx, ROW)
    z, core = col // 2, lax.rem(col, 2)
    place = row * 2 + core
    after, before = lax.rem(ctx + 1, ROW * ROWS), lax.rem(ctx + ROW * ROWS - 1, ROW * ROWS)

    def w_copy(group):
        at = pl.ds(pl.multiple_of(group * 256, 256), 256)
        return pltpu.make_async_copy(w_ref.at[:, :, at], wbuf.at[:, :, at], w_sem.at[group])

    late = [
        pltpu.make_async_copy(src, dst, in_sem.at[k])
        for k, (src, dst) in enumerate(((ld_hbm, ld_ref), (og_hbm, og_ref), (s0_hbm, s0_ref)))
    ]
    late[0].start()
    for group in range(4):
        w_copy(group).start()
    for copy in late[1:]:
        copy.start()
    x_copy = pltpu.make_async_copy(hid_ref, xext.at[pl.ds(HALO, TOK)], x_sem)
    x_copy.start()

    barrier = pltpu.get_barrier_semaphore()
    for step in range(1, ROW):
        mate = row * ROW + lax.rem(col + step, ROW)
        pl.semaphore_signal(barrier, inc=1, device_id=(mate, head), device_id_type=MESH)
    for step in range(1, ROW):
        mate = lax.rem(place + step, ROW)
        mate = mate // 2 * ROW + z * 2 + lax.rem(mate, 2)
        pl.semaphore_signal(barrier, inc=1, device_id=(mate, head), device_id_type=MESH)
    for step in range(1, 4):
        pl.semaphore_signal(barrier, inc=1, device_id=(ctx, lax.rem(head + step, 4)), device_id_type=MESH)
    for mate in (after, before):
        pl.semaphore_signal(barrier, inc=1, device_id=(mate, head), device_id_type=MESH)

    t, s = iota(0), iota(1)
    first = ctx * TOK
    seg_t, seg_s = jnp.zeros_like(t), jnp.zeros_like(s)
    seg_last, start = jnp.int32(0), jnp.int32(0)
    for doc in range(8):
        seg_t = jnp.where(t + first >= start, jnp.maximum(seg_t, start), seg_t)
        seg_s = jnp.where(s + first >= start, jnp.maximum(seg_s, start), seg_s)
        seg_last = jnp.where(first + TOK - 1 >= start, jnp.maximum(seg_last, start), seg_last)
        start = start + doc_ref[doc]
    same = seg_t == seg_s
    masks[0] = jnp.where(same & (t > s), 1.0, 0.0)
    masks[1] = jnp.where(same & (t >= s), 1.0, 0.0)
    masks[2] = jnp.where(seg_t < first, 1.0, 0.0)
    masks[3] = jnp.where(seg_t == seg_last, 1.0, 0.0)
    for offset in range(1, 4):
        masks[3 + offset] = jnp.where(t + first - offset >= seg_t, 1.0, 0.0)
    lead_last = jnp.where(seg_last < first, 1.0, 0.0)
    for h in range(HEADS):
        bet[h] = jnp.broadcast_to(beta_ref[h : h + 1, :], (TOK, TOK)).T

    pl.semaphore_wait(barrier, 2 * (ROW - 1) + 3 + 2)

    halo = pltpu.make_async_remote_copy(
        src_ref=hid_ref.at[pl.ds(TOK - HALO, HALO)], dst_ref=xext.at[pl.ds(0, HALO)],
        send_sem=halo_sem.at[0], recv_sem=halo_sem.at[1], device_id=(after, head), device_id_type=MESH,
    )
    halo.start()

    for tile in range(D // 128):
        ht_t[tile * 128 : tile * 128 + 128] = hid_ref[:, tile * 128 : tile * 128 + 128].astype(F32).T
    ht_t[D : D + 8] = jnp.zeros((8, TOK), F32)
    for axis in range(2):
        for owner in range(ROW):
            for piece in range(ROWS):
                slab = (piece * ROW + owner, owner // 2 * ROW + piece * 2 + owner % 2)[axis]
                rows = slice(slab * SLAB, slab * SLAB + PADDED)
                ht_send[axis, owner, piece * PADDED : piece * PADDED + PADDED] = ht_t[rows].astype(BF16)
    spot = (col, place)

    def tokens(j):
        return pl.ds(pl.multiple_of(j * TOK, TOK), TOK)

    def ht_copy(axis, step):
        mate = lax.rem(spot[axis] + step, ROW)
        device = (row * ROW + mate, mate // 2 * ROW + z * 2 + lax.rem(mate, 2))[axis]
        return pltpu.make_async_remote_copy(
            src_ref=ht_send.at[axis, mate], dst_ref=ht_recv.at[axis, :, tokens(spot[axis])],
            send_sem=ht_ssem.at[axis, step], recv_sem=ht_rsem.at[axis, step],
            device_id=(device, head), device_id_type=MESH,
        )

    for step in range(1, ROW):
        for axis in range(2):
            ht_copy(axis, step).start()
    for axis in range(2):
        ht_recv[axis, :, tokens(spot[axis])] = ht_send[axis, spot[axis]]

    below = (iota(0) >= iota(1)).astype(F32).astype(BF16)
    late[0].wait()
    for h in range(HEADS):
        summed = dot_exact_left(below, ld_ref[:, h * DK : h * DK + DK])
        mid = summed[63:64]
        grow[h], shrink[h] = jnp.exp(summed - mid), jnp.exp(mid - summed)
        edges[h, 0:1], edges[h, 1:2] = jnp.exp(mid), jnp.exp(summed[TOK - 1 :] - mid)

    x_copy.wait()
    halo.wait()

    def project(group, carry):
        w_copy(group).wait()
        wide = pl.ds(pl.multiple_of(group * 256, 256), 256)
        for p in range(3):
            made = jnp.dot(xext[...], wbuf[p, :, wide], preferred_element_type=F32)
            pe[p, :, wide] = made.astype(BF16).astype(F32)
        for half in range(2):
            h = group * 2 + half
            lanes = pl.ds(pl.multiple_of(h * DK, DK), DK)
            for p in range(3):
                mixed = pe[p, pl.ds(HALO, TOK), lanes] * conv_ref[p, 0:1, lanes]
                for offset in range(1, 4):
                    tap = pe[p, pl.ds(HALO - offset, TOK), lanes] * conv_ref[p, offset : offset + 1, lanes]
                    mixed = mixed + tap * masks[3 + offset]
                gate = 1.0 / (1.0 + jnp.exp(-mixed))
                active = mixed * gate
                dsil[p, h] = gate * (1.0 + mixed * (1.0 - gate))
                if p == 2:
                    val[h] = active
                else:
                    scale = lax.rsqrt(jnp.sum(active * active, axis=1, keepdims=True) + EPSILON)
                    norm[p, h] = active * scale
                    inv[p, h] = jnp.broadcast_to(scale, (TOK, DK))
        return carry

    lax.fori_loop(0, 4, project, 0)

    def mb_copy(h):
        return pltpu.make_async_remote_copy(
            src_ref=mb.at[h], dst_ref=rx.at[col], send_sem=mb_ssem.at[h], recv_sem=mb_rsem.at[col],
            device_id=(row * ROW + h, head), device_id_type=MESH,
        )

    batch = 8

    def transition(step, carry):
        heads = [step * batch + k for k in range(batch)]
        lanes = [pl.ds(pl.multiple_of(h * DK, DK), DK) for h in heads]
        ups, downs = [grow[h] for h in heads], [shrink[h] for h in heads]
        firsts, lasts = [edges[h, 0:1] for h in heads], [edges[h, 1:2] for h in heads]
        betas = [bet[h] for h in heads]
        grads_out = [og_ref[:, lane] for lane in lanes]
        keys = [norm[1, h] for h in heads]
        queries = [norm[0, h] * DK ** (-0.5) for h in heads]
        low = [k * x for k, x in zip(keys, downs)]
        high = [jnp.concatenate([k * x, q * x], axis=0) for k, q, x in zip(keys, queries, ups)]
        both = [dot3(a, b, NT) for a, b in zip(high, low)]
        ns = [jnp.where(masks[0] > 0, x[:TOK], 0.0) * b for x, b in zip(both, betas)]
        rs = [jnp.where(masks[1] > 0, x[TOK:], 0.0) for x in both]
        apart = iota(0) ^ iota(1)
        eye = (apart == 0).astype(F32)
        solved = [eye - jnp.where(apart == 1, n, 0.0) for n in ns]
        for level in range(1, 7):
            edge = [jnp.where((apart >> level) == 1, n, 0.0) for n in ns]
            edge = [dot3(e, x) for e, x in zip(edge, solved)]
            solved = [x - dot3(x, e) for e, x in zip(edge, solved)]
        lead = masks[2]
        ups0 = [x * e * lead for x, e in zip(ups, firsts)]
        ws = [dot1(x, b * k * up) for x, b, k, up in zip(solved, betas, keys, ups0)]
        xs = [q * up - dot1(r, w) for q, up, r, w in zip(queries, ups0, rs, ws)]
        ends = [x * last * masks[3] for x, last in zip(low, lasts)]
        moves = [
            (eye * (last * e * lead_last) - dot1(w, end, TN)).astype(BF16)
            for w, end, last, e in zip(ws, ends, lasts, firsts)
        ]
        owns = [dot1(x, og, TN).astype(BF16) for x, og in zip(xs, grads_out)]
        backs = [dot1(x, end, TN).astype(BF16) for x, end in zip(solved, ends)]
        for h, move, own, back, x, r in zip(heads, moves, owns, backs, solved, rs):
            mb[h, :, 0:DK], mb[h, :, DK:] = move, own
            tk[h], tinv[h], read[h] = back, x, r.astype(BF16)
        for h in heads:
            @pl.when(h != col)
            def _():
                mb_copy(h).start()
        return carry

    for copy in late[1:]:
        copy.wait()
    lax.fori_loop(0, HEADS // batch, transition, 0)
    rx[col] = mb[col]

    def shift_back(p, lane, dmix):
        t = iota(0)
        main = dmix * conv_ref[p, 0:1, lane]
        over = jnp.zeros((TOK, DK), F32)
        for offset in range(1, 4):
            shifted = dmix * masks[3 + offset] * conv_ref[p, offset : offset + 1, lane]
            shifted = pltpu.roll(shifted, TOK - offset, 0)
            inside = t < TOK - offset
            main = main + jnp.where(inside, shifted, 0.0)
            over = over + jnp.where(inside, 0.0, shifted)
        return main, over

    def keep(p, lane, main, over):
        own[p, :, lane] = main.astype(BF16)
        tail[p, :, lane] = main[TOK - HALO :]
        spill[p, :, lane] = over[TOK - 8 :]

    def unnorm(n, scale, grad):
        return scale * (grad - n * jnp.sum(n * grad, axis=1, keepdims=True))

    def local(step, carry):
        heads = [step * 4 + k for k in range(4)]
        lanes = [pl.ds(pl.multiple_of(h * DK, DK), DK) for h in heads]
        ogs = [og_ref[:, lane] for lane in lanes]
        ups, downs = [grow[h] for h in heads], [shrink[h] for h in heads]
        ups0 = [up * edges[h, 0:1] * masks[2] for h, up in zip(heads, ups)]
        normed = [norm[0, h] for h in heads]
        qs = [n * DK ** (-0.5) for n in normed]
        ks = [norm[1, h] for h in heads]
        states = [s0_ref[0, h].astype(BF16) for h in heads]
        ts = [tinv[h].astype(BF16) for h in heads]
        slopes, scales = [dsil[0, h] for h in heads], [inv[0, h] for h in heads]
        recalled = [dot1(k * up, state) for k, up, state in zip(ks, ups0, states)]
        fed = [dot1(read[h], og, TN) for h, og in zip(heads, ogs)]
        crossed = [dot1(og, state, NT) for og, state in zip(ogs, states)]
        wanted = [bet[h] * (val[h] - x) for h, x in zip(heads, recalled)]
        us = [dot1(t, x).astype(BF16) for t, x in zip(ts, wanted)]
        wls = [dot1(t, x, TN) for t, x in zip(ts, fed)]
        dreads = [jnp.where(masks[1] > 0, dot1(og, u, NT), 0.0).astype(BF16) for og, u in zip(ogs, us)]
        dqs = [dot1(x, k * down) * up + y * up0 for x, k, down, up, y, up0 in zip(dreads, ks, downs, ups, crossed, ups0)]
        dkms = [dot1(x, q * up, TN) for x, q, up in zip(dreads, qs, ups)]
        ggs = [q * dq for q, dq in zip(qs, dqs)]
        dmix = [unnorm(n, scale, dq * DK ** (-0.5)) * slope for n, scale, dq, slope in zip(normed, scales, dqs, slopes)]
        raw = [shift_back(0, lane, x) for lane, x in zip(lanes, dmix)]
        for h, lane, u, wlocal, km, g, (main, over) in zip(heads, lanes, us, wls, dkms, ggs, raw):
            uu[h], wl[h], dkm[h], gg[h] = u, wlocal, km, g
            keep(0, lane, main, over)
        return carry

    def spill_copy(at):
        p, first, width = ((0, 0, 1024), (1, 0, 512), (1, 512, 512))[at]
        block = (pl.ds(p, min(p + 1, 2)), slice(None), pl.ds(first, width))
        return pltpu.make_async_remote_copy(
            src_ref=spill.at[block], dst_ref=spill_in.at[block], send_sem=sp_sem.at[at, 0],
            recv_sem=sp_sem.at[at, 1], device_id=(before, head), device_id_type=MESH,
        )

    def add_spill(p, first, width, axis):
        at = pl.ds(first, width)
        low = tail[p, 8:16, at] + spill_in[p, :, at]
        own[p, TOK - HALO :, at] = jnp.concatenate([tail[p, 0:8, at], low], axis=0).astype(BF16)
        raws[p, tokens(spot[axis]), at] = own[p, :, at]

    def along(axis, step, other=0):
        to = lax.rem(core + other, 2)
        if axis == 0:
            return (row * ROW + lax.rem(z + step, 4) * 2 + to, head)
        return (lax.rem(row + step, 4) * ROW + z * 2 + to, head)

    def gather(unit, kind):
        p, first, width, axis = UNITS[unit]
        off = (0, 0, 3, 1, 0, 3, 1, 2)[kind]
        if kind == 2:
            at = pl.ds(first, width // 2)
        elif kind == 3:
            at = pl.ds(first + width // 2, width // 2)
        else:
            at = pl.ds(first, width)
        slot = lax.rem((z, row)[axis] + off, 4) * 2 + core
        block = raws.at[p, tokens(slot), at]
        to = along(axis, (1, 3, 1, 3, 0, 0, 0, 0)[kind], kind // 4)
        return pltpu.make_async_remote_copy(
            src_ref=block, dst_ref=block, send_sem=a_ssem.at[unit, kind], recv_sem=a_rsem.at[unit, kind],
            device_id=to, device_id_type=MESH,
        )

    def set_out(unit):
        add_spill(*UNITS[unit])
        for kind in (0, 1, 4):
            gather(unit, kind).start()

    def hand_on(unit):
        gather(unit, 0).wait_recv()
        gather(unit, 2).start()
        gather(unit, 5).start()
        gather(unit, 1).wait_recv()
        gather(unit, 3).start()
        gather(unit, 6).start()

    def part_copy(unit, step):
        p, first, width, axis = UNITS[unit]
        mate = lax.rem((row, z)[axis] + step, ROWS)
        at = pl.ds(first, width)
        return pltpu.make_async_remote_copy(
            src_ref=psend.at[p, pl.ds(pl.multiple_of(mate * PADDED, PADDED), PADDED), at],
            dst_ref=precv.at[p, step, :, at], send_sem=p_ssem.at[unit, step], recv_sem=p_rsem.at[unit, step],
            device_id=along(1 - axis, step), device_id_type=MESH,
        )

    def finish(unit):
        p, first, width, axis = UNITS[unit]
        gather(unit, 2).wait_recv()
        gather(unit, 3).wait_recv()
        gather(unit, 7).start()
        for kind in (4, 5, 6, 7):
            gather(unit, kind).wait_recv()

        def product(tile, carry):
            at = pl.ds(pl.multiple_of(first + tile * 256, 256), 256)
            made = jnp.dot(ht_recv[axis], raws[p, :, at], preferred_element_type=F32)
            psend[p, :, at] = made.astype(BF16)
            part[:, at] = made
            return carry

        lax.fori_loop(0, width // 256, product, 0)
        for step in range(1, ROWS):
            part_copy(unit, step).start()
        at = pl.ds(first, width)
        wg_ref[p, :, at] = part[pl.ds(pl.multiple_of((row, z)[axis] * PADDED, 8), SLAB), at]

    def receive(unit):
        p, first, width, axis = UNITS[unit]
        at = pl.ds(first, width)
        total = wg_ref[p, :, at]
        for step in range(1, ROWS):
            part_copy(unit, step).wait_recv()
            total = total + precv[p, step, :, at].astype(F32)[:SLAB]
        wg_ref[p, :, at] = total

    def input_part(low, high):
        def one(tile, carry):
            at = pl.ds(pl.multiple_of(tile * 256, 256), 256)
            total = jnp.zeros((TOK, 256), F32) if low == 0 else ipart[:, at]
            for p in range(low, high):
                mine = own[p]
                total = total + lax.dot_general(mine, wbuf[p, at, :], NT, preferred_element_type=F32)
            ipart[:, at] = total
            if high == 3:
                isend[:, at] = total.astype(BF16)
            return carry

        lax.fori_loop(0, D // 256, one, 0)

    def input_copy(step):
        mate = lax.rem(head + step, 4)
        return pltpu.make_async_remote_copy(
            src_ref=isend.at[pl.ds(pl.multiple_of(mate * 32, 32), 32)], dst_ref=irecv.at[step],
            send_sem=i_ssem.at[step], recv_sem=i_rsem.at[step], device_id=(ctx, mate), device_id_type=MESH,
        )

    lax.fori_loop(0, HEADS // 4, local, 0)
    spill_copy(0).start()

    for j in range(ROW):
        @pl.when(j != col)
        def _():
            pltpu.make_async_remote_copy(
                src_ref=mb.at[j], dst_ref=rx.at[j], send_sem=mb_ssem.at[j], recv_sem=mb_rsem.at[j],
                device_id=(row * ROW + j, head), device_id_type=MESH,
            ).wait_recv()

    spill_copy(0).wait_recv()
    set_out(0)
    set_out(1)

    def compose(m, x, b):
        hi, lo = split(x)
        out = jnp.dot(m, jnp.concatenate([hi, lo], axis=1), preferred_element_type=F32)
        n = x.shape[1]
        return out[:, :n] + out[:, n:] + b

    half = ROW // 2
    zeros = jnp.zeros((DK, DK), F32)
    ends = [rx[half - 1].astype(F32), rx[ROW - 1].astype(F32)]
    for j in range(half - 2, -1, -1):
        for k in range(2):
            at = k * half + j
            pc[at] = ends[k]
            b = jnp.concatenate([zeros, rx[at, :, DK:].astype(F32)], axis=1)
            ends[k] = compose(rx[at, :, 0:DK], ends[k], b)
    b = jnp.concatenate([zeros, ends[0][:, DK:]], axis=1)
    tot[...] = (dot3(ends[0][:, 0:DK], ends[1]) + b).astype(BF16)

    def ry_copy(step):
        mate = lax.rem(row + step, ROWS) * ROW + col
        return pltpu.make_async_remote_copy(
            src_ref=tot, dst_ref=ry.at[ROWS - step], send_sem=ry_ssem.at[step], recv_sem=ry_rsem.at[step],
            device_id=(mate, head), device_id_type=MESH,
        )

    for step in range(1, ROWS):
        @pl.when(row + step >= ROWS)
        def _():
            ry_copy(step).start()

    hand_on(0)
    hand_on(1)
    for axis in range(2):
        for step in range(1, ROW):
            ht_copy(axis, step).wait()
    carry_in[...] = zeros
    for k in range(ROWS - 1, 0, -1):
        @pl.when(row + k < ROWS)
        def _():
            ry_copy(ROWS - k).wait_recv()
            carry_in[...] = compose(ry[k, :, 0:DK], carry_in[...], ry[k, :, DK:].astype(F32))

    total = carry_in[...]

    def ds_copy(j):
        return pltpu.make_async_remote_copy(
            src_ref=ds.at[j], dst_ref=rd.at[col], send_sem=ds_ssem.at[j], recv_sem=ds_rsem.at[col],
            device_id=(row * ROW + j, head), device_id_type=MESH,
        )

    middle = dot3(ends[1][:, 0:DK], total) + ends[1][:, DK:]
    entries = [middle.astype(BF16), total.astype(BF16)]
    for j in range(ROW):
        if j % half == half - 1:
            ds[j] = entries[j // half]
        else:
            ds[j] = (dot1(pc[j, :, 0:DK], entries[j // half]) + pc[j, :, DK:]).astype(BF16)

        @pl.when(j != col)
        def _():
            ds_copy(j).start()

    rd[col] = ds[col]

    finish(0)
    finish(1)
    input_part(0, 1)

    for j in range(ROW):
        @pl.when(j != col)
        def _():
            pltpu.make_async_remote_copy(
                src_ref=ds.at[j], dst_ref=rd.at[j], send_sem=ds_ssem.at[j], recv_sem=ds_rsem.at[j],
                device_id=(row * ROW + j, head), device_id_type=MESH,
            ).wait_recv()

    def carried(step, carry):
        heads = [step * 4 + k for k in range(4)]
        lanes = [pl.ds(pl.multiple_of(h * DK, DK), DK) for h in heads]
        above = (iota(1) >= iota(0)).astype(F32).astype(BF16)
        ones = jnp.ones((8, DK), BF16)
        lead = masks[2]
        ups, downs = [grow[h] for h in heads], [shrink[h] for h in heads]
        firsts, lasts = [edges[h, 0:1] for h in heads], [edges[h, 1:2] for h in heads]
        ks = [norm[1, h] for h in heads]
        nexts = [rd[h] for h in heads]
        states = [s0_ref[0, h] for h in heads]
        us = [uu[h] for h in heads]
        read_dkm, read_gg = [dkm[h] for h in heads], [gg[h] for h in heads]
        slopes = [(dsil[1, h], dsil[2, h]) for h in heads]
        scales = [inv[1, h] for h in heads]
        bws = [bet[h] * (wl[h] + dot1(tk[h], x)) for h, x in zip(heads, nexts)]
        das = [jnp.where(masks[0] > 0, -dot1(bw, u, NT), 0.0).astype(BF16) for bw, u in zip(bws, us)]
        olds = [dot1(bw * lead, state, NT) * e for bw, state, e in zip(bws, states, firsts)]
        dkus = [dot1(da, k * down) - old for da, k, down, old in zip(das, ks, downs, olds)]
        dkms = [x + dot1(da, k * up, TN) for x, da, k, up in zip(read_dkm, das, ks, ups)]
        dends = [dot1(u, x, NT) * e * masks[3] for u, x, e in zip(us, nexts, lasts)]
        risings = [x * up for x, up in zip(dkus, ups)]
        endings = [x * down for x, down in zip(dends, downs)]
        fallings = [x * down + y for x, down, y in zip(dkms, downs, endings)]
        dmix = [
            unnorm(k, scale, x + y) * slope[0]
            for k, scale, x, y, slope in zip(ks, scales, risings, fallings, slopes)
        ]
        raw1 = [shift_back(1, lane, x) for lane, x in zip(lanes, dmix)]
        raw2 = [shift_back(2, lane, bw * slope[1]) for lane, bw, slope in zip(lanes, bws, slopes)]
        for lane, one, two in zip(lanes, raw1, raw2):
            keep(1, lane, *one)
            keep(2, lane, *two)
        dgs = [g + k * (x - y) for g, k, x, y in zip(read_gg, ks, risings, fallings)]
        crossed = [split(state * x.astype(F32) * lead_last) for state, x in zip(states, nexts)]
        extras = [dot1(ones, ch, NT) + dot1(ones, cl, NT) for ch, cl in crossed]
        extras = [
            x[0:1] * e * last + jnp.sum(k * y, axis=0, keepdims=True)
            for x, e, last, k, y in zip(extras, firsts, lasts, ks, endings)
        ]
        dlds = [dot_exact_left(above, dg) + x for dg, x in zip(dgs, extras)]
        for lane, x in zip(lanes, dlds):
            dld_ref[:, lane] = x
        return carry

    carried(0, 0)
    spill_copy(1).start()
    carried(1, 0)
    spill_copy(2).start()
    spill_copy(1).wait_recv()
    set_out(2)
    set_out(3)
    spill_copy(2).wait_recv()
    set_out(4)
    set_out(5)
    hand_on(2)
    hand_on(3)
    input_part(1, 3)
    for step in range(1, 4):
        input_copy(step).start()
    finish(2)
    finish(3)
    hand_on(4)
    hand_on(5)
    receive(0)
    receive(1)
    finish(4)
    finish(5)
    for step in range(1, 4):
        input_copy(step).wait_recv()
    total = ipart[pl.ds(pl.multiple_of(head * 32, 32), 32), :]
    for step in range(1, 4):
        total = total + irecv[step].astype(F32)
    ig_ref[...] = total.astype(BF16)
    for unit in range(2, len(UNITS)):
        receive(unit)

    for at in range(3):
        spill_copy(at).wait_send()
    for step in range(1, ROWS):
        input_copy(step).wait_send()

        @pl.when(row + step >= ROWS)
        def _():
            ry_copy(step).wait_send()

    for j in range(ROW):
        @pl.when(j != col)
        def _():
            mb_copy(j).wait_send()
            ds_copy(j).wait_send()
    for unit in range(len(UNITS)):
        for kind in range(8):
            gather(unit, kind).wait_send()
        for step in range(1, ROWS):
            part_copy(unit, step).wait_send()


def chain(doc_lengths, hidden, proj_weight, conv_weight, log_decay, write_beta, saved_state, output_grad):
    vm = pl.BlockSpec(memory_space=pltpu.VMEM)
    hbm = pl.BlockSpec(memory_space=pl.ANY)
    sq = (HEADS, TOK, DK)
    dma = pltpu.SemaphoreType.DMA
    return pl.pallas_call(
        chain_kernel,
        out_shape=(
            jax.ShapeDtypeStruct((3, SLAB, HEADS * DK), F32),
            jax.ShapeDtypeStruct((32, D), BF16),
            jax.ShapeDtypeStruct((TOK, HEADS * DK), F32),
        ),
        in_specs=[pl.BlockSpec(memory_space=pltpu.SMEM), vm, hbm, vm, hbm, vm, hbm, hbm],
        out_specs=(vm, vm, vm),
        scratch_shapes=[
            pltpu.VMEM((TOK, HEADS * DK), F32),
            pltpu.VMEM((1,) + sq, F32),
            pltpu.VMEM((TOK, HEADS * DK), BF16),
            pltpu.VMEM((HALO + TOK, D), BF16),
            pltpu.VMEM((3, D, HEADS * DK), BF16),
            pltpu.VMEM((3, HALO + TOK, HEADS * DK), F32),
            pltpu.VMEM((D + 8, TOK), F32),
            pltpu.VMEM((2, ROW, ROWS * PADDED, TOK), BF16),
            pltpu.VMEM((2, ROWS * PADDED, ROW * TOK), BF16),
            pltpu.VMEM((2,) + sq, F32),
            pltpu.VMEM(sq, F32),
            pltpu.VMEM((2,) + sq, F32),
            pltpu.VMEM((3,) + sq, F32),
            pltpu.VMEM((7, TOK, TOK), F32),
            pltpu.VMEM(sq, F32),
            pltpu.VMEM(sq, F32),
            pltpu.VMEM(sq, F32),
            pltpu.VMEM((HEADS, 8, DK), F32),
            pltpu.VMEM(sq, F32),
            pltpu.VMEM(sq, BF16),
            pltpu.VMEM((HEADS, DK, 2 * DK), BF16),
            pltpu.VMEM((ROW, DK, 2 * DK), BF16),
            pltpu.VMEM((ROW, DK, 2 * DK), F32),
            pltpu.VMEM((DK, 2 * DK), BF16),
            pltpu.VMEM((ROWS, DK, 2 * DK), BF16),
            pltpu.VMEM((DK, DK), F32),
            pltpu.VMEM((ROW, DK, DK), BF16),
            pltpu.VMEM((HEADS, DK, DK), BF16),
            pltpu.VMEM(sq, BF16),
            pltpu.VMEM(sq, F32),
            pltpu.VMEM(sq, BF16),
            pltpu.VMEM(sq, F32),
            pltpu.VMEM(sq, F32),
            pltpu.VMEM((3, HALO, HEADS * DK), F32),
            pltpu.VMEM((3, 8, HEADS * DK), F32),
            pltpu.VMEM((3, 8, HEADS * DK), F32),
            pltpu.VMEM((3, TOK, HEADS * DK), BF16),
            pltpu.VMEM((3, ROW * TOK, HEADS * DK), BF16),
            pltpu.VMEM((ROWS * PADDED, HEADS * DK), F32),
            pltpu.VMEM((3, ROWS * PADDED, HEADS * DK), BF16),
            pltpu.VMEM((3, ROWS, PADDED, HEADS * DK), BF16),
            pltpu.VMEM((TOK, D), F32),
            pltpu.VMEM((TOK, D), BF16),
            pltpu.VMEM((4, 32, D), BF16),
            dma((3,)), dma((4,)), dma, dma((2,)), dma((2, ROW)), dma((2, ROW)), dma((ROW,)), dma((ROW,)),
            dma((ROWS,)), dma((ROWS,)), dma((ROW,)), dma((ROW,)), dma((3, 2)),
            dma((len(UNITS), 8)), dma((len(UNITS), 8)), dma((len(UNITS), ROWS)), dma((len(UNITS), ROWS)), dma((4,)), dma((4,)),
        ],
        compiler_params=pltpu.CompilerParams(
            collective_id=0, has_side_effects=True, vmem_limit_bytes=56 * 1024 * 1024
        ),
        cost_estimate=pl.CostEstimate(flops=8_000_000_000, bytes_accessed=18_000_000, transcendentals=1_000_000),
        name="chain",
    )(doc_lengths, hidden, proj_weight, conv_weight, log_decay, write_beta.T, saved_state, output_grad)


def settle_kernel(wg_ref, ig_ref, dld_ref, wg_out, ig_out, dld_out, wg, ig, dld, sems):
    moves = ((wg_ref, wg, wg_out), (dld_ref, dld, dld_out), (ig_ref, ig, ig_out))
    inward = [pltpu.make_async_copy(src, mid, sems.at[0, k]) for k, (src, mid, dst) in enumerate(moves)]
    outward = [pltpu.make_async_copy(mid, dst, sems.at[1, k]) for k, (src, mid, dst) in enumerate(moves)]
    for copy in inward:
        copy.start()
    for arrived, copy in zip(inward, outward):
        arrived.wait()
        copy.start()
    for copy in outward:
        copy.wait()


def settle(*arrays):
    anywhere = pl.BlockSpec(memory_space=pl.ANY)
    return pl.pallas_call(
        settle_kernel,
        out_shape=tuple(jax.ShapeDtypeStruct(a.shape, a.dtype) for a in arrays),
        in_specs=[anywhere] * 3,
        out_specs=(anywhere,) * 3,
        scratch_shapes=[pltpu.VMEM(a.shape, a.dtype) for a in arrays] + [pltpu.SemaphoreType.DMA((2, 3))],
        name="settle",
    )(*arrays)


def body(hidden, proj_weight, conv_weight, log_decay, write_beta, saved_state, output_grad, doc_lengths):
    weight_grads, input_grad, decay_grad = settle(
        *chain(doc_lengths, hidden, proj_weight, conv_weight, log_decay, write_beta, saved_state, output_grad)
    )
    return (jnp.transpose(weight_grads, (1, 0, 2)), input_grad, decay_grad)


def solution(mesh):
    return jax.shard_map(
        body,
        mesh=mesh,
        in_specs=(
            P("ctx", None),
            P(None, None, "head"),
            P(None, None, "head"),
            P("ctx", "head"),
            P("ctx", "head"),
            P("ctx", "head", None, None),
            P("ctx", "head"),
            P(),
        ),
        out_specs=(P("ctx", None, "head"), P(("ctx", "head"), None), P("ctx", "head")),
        check_vma=False,
    )
```

time: 113 us -> 82.9 us (0.73)
  Pallas kernels: 106 us -> 82 us
  local copies, waits for them, and re-layouts: 5.97 us -> 0 us
    pallas_call x2, Pallas kernels: 106 us -> 82 us  [the longest x1 79.6 us: chain(): pl.pallas_call(chain_kernel, out_shape=(jax.ShapeDtypeStruct((3, SLAB, HE...]
    unnamed x6 -> x0, local copies, waits for them, and re-layouts: 5.97 us -> none
where the time goes in v2:
time: 82.9 us; the launch traced here: 82.8 us
  Pallas kernels  82 us (99%)
    pallas_call x1, Pallas kernels, chain(): pl.pallas_call(chain_kernel, out_shape=(jax.ShapeDtypeStruct((3, SLAB, HE...  79.6 us
    pallas_call x1, Pallas kernels, settle(): pl.pallas_call(settle_kernel, out_shape=tuple((jax.ShapeDtypeStruct(a.sha...  2.34 us

profile of v2, /device:TPU:1, one launch (start us, length us, event | category | flops | bytes accessed | tf_op | source)
XLA Modules:
  0.0 82.8 jit_solution(10293522584836189465)
XLA Ops:
  0.6 79.6 %chain.1 = (f32[3,72,1024]{2,1,0:T(8,128)}, bf16[32,2304]{1,0:T(8,128)(2,1)}, f32[128,1024]{1,0:T(8,128)}) custom-call(s32[8]{0:T(128)} %doc_ref.1, bf16[128,2304]{1,0:T(8,128)(2,1)} %hid_ref.1, bf16[3,2304,1024]{2,1,0:T(8,128)(2,1)} %w_ref.1, f32[3,4,1024]{2,1,0:T(4,128)} %conv_ref.1, f32[128,1024]{1,0:T(8,128)} %ld_hbm.1, f32[8,128]{1,0:T(8,128)} %bitcast.3, ...), custom_call_target="tpu_custom_call" | custom-call | flops 8000000000 | bytes 18000000 | tf_op jit(solution)/shard_map/chain/pallas_call | solution.py:602
  80.3 2.3 %settle.1 = (f32[3,72,1024]{2,1,0:T(8,128)}, bf16[32,2304]{1,0:T(8,128)(2,1)}, f32[128,1024]{1,0:T(8,128)}) custom-call(f32[3,72,1024]{2,1,0:T(8,128)} %get-tuple-element.9.wg_ref, bf16[32,2304]{1,0:T(8,128)(2,1)} %get-tuple-element.10.ig_ref, f32[128,1024]{1,0:T(8,128)} %get-tuple-element.11.dld_ref), custom_call_target="tpu_custom_call" | custom-call | tf_op jit(solution)/shard_map/settle/pallas_call | solution.py:683

commit v3 on v2

--- a/solution.py
+++ b/solution.py
@@ -12,7 +12,7 @@
 EPSILON = 1e-06
 HEADS, TOK, DK, D = 8, 128, 128, 2304
 ROW, ROWS = 8, 4
-SLAB, PADDED = 72, 80
+SLAB, HALF = 72, 256
 HALO = 16
 NN, NT, TN = (((1,), (0,)), ((), ())), (((1,), (1,)), ((), ())), (((0,), (0,)), ((), ()))
 
@@ -34,6 +34,13 @@
     return lax.dot_general(left, right, form, preferred_element_type=F32)
 
 
+def two_pass(a, b):
+    ah, al = split(a)
+    return lax.dot_general(
+        jnp.concatenate([ah, al], axis=1), jnp.concatenate([b, b], axis=0), NN, preferred_element_type=F32
+    )
+
+
 def dot_exact_left(a, b):
     bh, bl = split(b)
     return lax.dot_general(
@@ -50,6 +57,7 @@
 
 
 UNITS = ((0, 0, 512, 0), (0, 512, 512, 1), (1, 0, 512, 0), (2, 0, 512, 1), (1, 512, 512, 0), (2, 512, 512, 1))
+FAR_FIRST = (4, 5, 3, 2, 6, 7, 1)
 
 
 def chain_kernel(
@@ -126,13 +134,13 @@
 
     for tile in range(D // 128):
         ht_t[tile * 128 : tile * 128 + 128] = hid_ref[:, tile * 128 : tile * 128 + 128].astype(F32).T
-    ht_t[D : D + 8] = jnp.zeros((8, TOK), F32)
     for axis in range(2):
         for owner in range(ROW):
-            for piece in range(ROWS):
-                slab = (piece * ROW + owner, owner // 2 * ROW + piece * 2 + owner % 2)[axis]
-                rows = slice(slab * SLAB, slab * SLAB + PADDED)
-                ht_send[axis, owner, piece * PADDED : piece * PADDED + PADDED] = ht_t[rows].astype(BF16)
+            slabs = [
+                (piece * ROW + owner, owner // 2 * ROW + piece * 2 + owner % 2)[axis] for piece in range(ROWS)
+            ]
+            rows = [ht_t[slab * SLAB : slab * SLAB + SLAB] for slab in slabs]
+            ht_send[axis, owner] = jnp.concatenate(rows, axis=0).astype(BF16)
     spot = (col, place)
 
     def tokens(j):
@@ -222,7 +230,7 @@
             solved = [x - dot3(x, e) for e, x in zip(edge, solved)]
         lead = masks[2]
         ups0 = [x * e * lead for x, e in zip(ups, firsts)]
-        ws = [dot1(x, b * k * up) for x, b, k, up in zip(solved, betas, keys, ups0)]
+        ws = [dot3(x, b * k * up) for x, b, k, up in zip(solved, betas, keys, ups0)]
         xs = [q * up - dot1(r, w) for q, up, r, w in zip(queries, ups0, rs, ws)]
         ends = [x * last * masks[3] for x, last in zip(low, lasts)]
         moves = [
@@ -230,14 +238,12 @@
             for w, end, last, e in zip(ws, ends, lasts, firsts)
         ]
         owns = [dot1(x, og, TN).astype(BF16) for x, og in zip(xs, grads_out)]
-        backs = [dot1(x, end, TN).astype(BF16) for x, end in zip(solved, ends)]
+        backs = [dot3(x, end, TN) for x, end in zip(solved, ends)]
         for h, move, own, back, x, r in zip(heads, moves, owns, backs, solved, rs):
             mb[h, :, 0:DK], mb[h, :, DK:] = move, own
             tk[h], tinv[h], read[h] = back, x, r.astype(BF16)
-        for h in heads:
-            @pl.when(h != col)
-            def _():
-                mb_copy(h).start()
+        for step in FAR_FIRST:
+            mb_copy(lax.rem(col + step, ROW)).start()
         return carry
 
     for copy in late[1:]:
@@ -274,19 +280,22 @@
         normed = [norm[0, h] for h in heads]
         qs = [n * DK ** (-0.5) for n in normed]
         ks = [norm[1, h] for h in heads]
-        states = [s0_ref[0, h].astype(BF16) for h in heads]
-        ts = [tinv[h].astype(BF16) for h in heads]
+        states = [s0_ref[0, h] for h in heads]
+        ts = [tinv[h] for h in heads]
         slopes, scales = [dsil[0, h] for h in heads], [inv[0, h] for h in heads]
-        recalled = [dot1(k * up, state) for k, up, state in zip(ks, ups0, states)]
+        recalled = [dot3(k * up, state) for k, up, state in zip(ks, ups0, states)]
         fed = [dot1(read[h], og, TN) for h, og in zip(heads, ogs)]
         crossed = [dot1(og, state, NT) for og, state in zip(ogs, states)]
         wanted = [bet[h] * (val[h] - x) for h, x in zip(heads, recalled)]
-        us = [dot1(t, x).astype(BF16) for t, x in zip(ts, wanted)]
-        wls = [dot1(t, x, TN) for t, x in zip(ts, fed)]
+        us = [dot3(t, x).astype(BF16) for t, x in zip(ts, wanted)]
+        wls = [dot3(t, x, TN) for t, x in zip(ts, fed)]
         dreads = [jnp.where(masks[1] > 0, dot1(og, u, NT), 0.0).astype(BF16) for og, u in zip(ogs, us)]
-        dqs = [dot1(x, k * down) * up + y * up0 for x, k, down, up, y, up0 in zip(dreads, ks, downs, ups, crossed, ups0)]
-        dkms = [dot1(x, q * up, TN) for x, q, up in zip(dreads, qs, ups)]
-        ggs = [q * dq for q, dq in zip(qs, dqs)]
+        kms = [(k * down).astype(BF16) for k, down in zip(ks, downs)]
+        qus = [(q * up).astype(BF16) for q, up in zip(qs, ups)]
+        dqus = [dot1(x, km) for x, km in zip(dreads, kms)]
+        dqs = [x * up + y * up0 for x, up, y, up0 in zip(dqus, ups, crossed, ups0)]
+        dkms = [dot1(x, qu, TN) for x, qu in zip(dreads, qus)]
+        ggs = [qu.astype(F32) * x + q * up0 * y for qu, x, q, up0, y in zip(qus, dqus, qs, ups0, crossed)]
         dmix = [unnorm(n, scale, dq * DK ** (-0.5)) * slope for n, scale, dq, slope in zip(normed, scales, dqs, slopes)]
         raw = [shift_back(0, lane, x) for lane, x in zip(lanes, dmix)]
         for h, lane, u, wlocal, km, g, (main, over) in zip(heads, lanes, us, wls, dkms, ggs, raw):
@@ -347,42 +356,41 @@
     def part_copy(unit, step):
         p, first, width, axis = UNITS[unit]
         mate = lax.rem((row, z)[axis] + step, ROWS)
-        at = pl.ds(first, width)
         return pltpu.make_async_remote_copy(
-            src_ref=psend.at[p, pl.ds(pl.multiple_of(mate * PADDED, PADDED), PADDED), at],
-            dst_ref=precv.at[p, step, :, at], send_sem=p_ssem.at[unit, step], recv_sem=p_rsem.at[unit, step],
+            src_ref=psend.at[unit, mate], dst_ref=precv.at[unit, step],
+            send_sem=p_ssem.at[unit, step], recv_sem=p_rsem.at[unit, step],
             device_id=along(1 - axis, step), device_id_type=MESH,
         )
 
-    def finish(unit):
-        p, first, width, axis = UNITS[unit]
+    def share(unit):
         gather(unit, 2).wait_recv()
         gather(unit, 3).wait_recv()
         gather(unit, 7).start()
+
+    def finish(unit):
+        p, first, width, axis = UNITS[unit]
         for kind in (4, 5, 6, 7):
             gather(unit, kind).wait_recv()
-
-        def product(tile, carry):
-            at = pl.ds(pl.multiple_of(first + tile * 256, 256), 256)
-            made = jnp.dot(ht_recv[axis], raws[p, :, at], preferred_element_type=F32)
-            psend[p, :, at] = made.astype(BF16)
-            part[:, at] = made
-            return carry
-
-        lax.fori_loop(0, width // 256, product, 0)
+        made = [
+            jnp.dot(ht_recv[axis], raws[p, :, first + at : first + at + HALF], preferred_element_type=F32)
+            for at in (0, HALF)
+        ]
+        for piece in range(ROWS):
+            rows = slice(piece * SLAB, piece * SLAB + SLAB)
+            block = jnp.concatenate([made[0][rows], made[1][rows]], axis=0)
+            psend[unit, piece] = block.astype(BF16)
+            part[unit, piece] = block
         for step in range(1, ROWS):
             part_copy(unit, step).start()
-        at = pl.ds(first, width)
-        wg_ref[p, :, at] = part[pl.ds(pl.multiple_of((row, z)[axis] * PADDED, 8), SLAB), at]
 
     def receive(unit):
         p, first, width, axis = UNITS[unit]
-        at = pl.ds(first, width)
-        total = wg_ref[p, :, at]
+        total = part[unit, (row, z)[axis]]
         for step in range(1, ROWS):
             part_copy(unit, step).wait_recv()
-            total = total + precv[p, step, :, at].astype(F32)[:SLAB]
-        wg_ref[p, :, at] = total
+            total = total + precv[unit, step].astype(F32)
+        wg_ref[p, :, first : first + HALF] = total[:SLAB]
+        wg_ref[p, :, first + HALF : first + 2 * HALF] = total[SLAB:]
 
     def input_part(low, high):
         def one(tile, carry):
@@ -477,24 +485,24 @@
             ds[j] = entries[j // half]
         else:
             ds[j] = (dot1(pc[j, :, 0:DK], entries[j // half]) + pc[j, :, DK:]).astype(BF16)
-
-        @pl.when(j != col)
-        def _():
-            ds_copy(j).start()
-
+    for step in FAR_FIRST:
+        ds_copy(lax.rem(col + step, ROW)).start()
     rd[col] = ds[col]
 
+    share(0)
+    share(1)
     finish(0)
     finish(1)
     input_part(0, 1)
 
-    for j in range(ROW):
-        @pl.when(j != col)
-        def _():
-            pltpu.make_async_remote_copy(
-                src_ref=ds.at[j], dst_ref=rd.at[j], send_sem=ds_ssem.at[j], recv_sem=ds_rsem.at[j],
-                device_id=(row * ROW + j, head), device_id_type=MESH,
-            ).wait_recv()
+    def returned(first, last):
+        for j in range(first, last):
+            @pl.when(j != col)
+            def _():
+                pltpu.make_async_remote_copy(
+                    src_ref=ds.at[j], dst_ref=rd.at[j], send_sem=ds_ssem.at[j], recv_sem=ds_rsem.at[j],
+                    device_id=(row * ROW + j, head), device_id_type=MESH,
+                ).wait_recv()
 
     def carried(step, carry):
         heads = [step * 4 + k for k in range(4)]
@@ -511,13 +519,15 @@
         read_dkm, read_gg = [dkm[h] for h in heads], [gg[h] for h in heads]
         slopes = [(dsil[1, h], dsil[2, h]) for h in heads]
         scales = [inv[1, h] for h in heads]
-        bws = [bet[h] * (wl[h] + dot1(tk[h], x)) for h, x in zip(heads, nexts)]
+        bws = [bet[h] * (wl[h] + two_pass(tk[h], x)) for h, x in zip(heads, nexts)]
         das = [jnp.where(masks[0] > 0, -dot1(bw, u, NT), 0.0).astype(BF16) for bw, u in zip(bws, us)]
         olds = [dot1(bw * lead, state, NT) * e for bw, state, e in zip(bws, states, firsts)]
-        dkus = [dot1(da, k * down) - old for da, k, down, old in zip(das, ks, downs, olds)]
-        dkms = [x + dot1(da, k * up, TN) for x, da, k, up in zip(read_dkm, das, ks, ups)]
+        kms = [(k * down).astype(BF16) for k, down in zip(ks, downs)]
+        kus = [(k * up).astype(BF16) for k, up in zip(ks, ups)]
+        dkus = [dot1(da, km) for da, km in zip(das, kms)]
+        dkms = [x + dot1(da, ku, TN) for x, da, ku in zip(read_dkm, das, kus)]
         dends = [dot1(u, x, NT) * e * masks[3] for u, x, e in zip(us, nexts, lasts)]
-        risings = [x * up for x, up in zip(dkus, ups)]
+        risings = [(x - old) * up for x, old, up in zip(dkus, olds, ups)]
         endings = [x * down for x, down in zip(dends, downs)]
         fallings = [x * down + y for x, down, y in zip(dkms, downs, endings)]
         dmix = [
@@ -529,7 +539,10 @@
         for lane, one, two in zip(lanes, raw1, raw2):
             keep(1, lane, *one)
             keep(2, lane, *two)
-        dgs = [g + k * (x - y) for g, k, x, y in zip(read_gg, ks, risings, fallings)]
+        dgs = [
+            g + ku.astype(F32) * x - km.astype(F32) * y - k * (old * up + end)
+            for g, ku, x, km, y, k, old, up, end in zip(read_gg, kus, dkus, kms, dkms, ks, olds, ups, endings)
+        ]
         crossed = [split(state * x.astype(F32) * lead_last) for state, x in zip(states, nexts)]
         extras = [dot1(ones, ch, NT) + dot1(ones, cl, NT) for ch, cl in crossed]
         extras = [
@@ -541,8 +554,10 @@
             dld_ref[:, lane] = x
         return carry
 
+    returned(0, 4)
     carried(0, 0)
     spill_copy(1).start()
+    returned(4, 8)
     carried(1, 0)
     spill_copy(2).start()
     spill_copy(1).wait_recv()
@@ -556,10 +571,14 @@
     input_part(1, 3)
     for step in range(1, 4):
         input_copy(step).start()
+    hand_on(4)
+    hand_on(5)
+    share(2)
+    share(3)
     finish(2)
     finish(3)
-    hand_on(4)
-    hand_on(5)
+    share(4)
+    share(5)
     receive(0)
     receive(1)
     finish(4)
@@ -615,9 +634,9 @@
             pltpu.VMEM((HALO + TOK, D), BF16),
             pltpu.VMEM((3, D, HEADS * DK), BF16),
             pltpu.VMEM((3, HALO + TOK, HEADS * DK), F32),
-            pltpu.VMEM((D + 8, TOK), F32),
-            pltpu.VMEM((2, ROW, ROWS * PADDED, TOK), BF16),
-            pltpu.VMEM((2, ROWS * PADDED, ROW * TOK), BF16),
+            pltpu.VMEM((D, TOK), F32),
+            pltpu.VMEM((2, ROW, ROWS * SLAB, TOK), BF16),
+            pltpu.VMEM((2, ROWS * SLAB, ROW * TOK), BF16),
             pltpu.VMEM((2,) + sq, F32),
             pltpu.VMEM(sq, F32),
             pltpu.VMEM((2,) + sq, F32),
@@ -639,7 +658,7 @@
             pltpu.VMEM((HEADS, DK, DK), BF16),
             pltpu.VMEM(sq, BF16),
             pltpu.VMEM(sq, F32),
-            pltpu.VMEM(sq, BF16),
+            pltpu.VMEM(sq, F32),
             pltpu.VMEM(sq, F32),
             pltpu.VMEM(sq, F32),
             pltpu.VMEM((3, HALO, HEADS * DK), F32),
@@ -647,9 +666,9 @@
             pltpu.VMEM((3, 8, HEADS * DK), F32),
             pltpu.VMEM((3, TOK, HEADS * DK), BF16),
             pltpu.VMEM((3, ROW * TOK, HEADS * DK), BF16),
-            pltpu.VMEM((ROWS * PADDED, HEADS * DK), F32),
-            pltpu.VMEM((3, ROWS * PADDED, HEADS * DK), BF16),
-            pltpu.VMEM((3, ROWS, PADDED, HEADS * DK), BF16),
+            pltpu.VMEM((len(UNITS), ROWS, 2 * SLAB, HALF), F32),
+            pltpu.VMEM((len(UNITS), ROWS, 2 * SLAB, HALF), BF16),
+            pltpu.VMEM((len(UNITS), ROWS, 2 * SLAB, HALF), BF16),
             pltpu.VMEM((TOK, D), F32),
             pltpu.VMEM((TOK, D), BF16),
             pltpu.VMEM((4, 32, D), BF16),

time: 82.9 us -> 73.3 us (0.88)
  Pallas kernels: 82 us -> 72.3 us
    pallas_call x1, Pallas kernels: 79.6 us -> 70 us  [chain(): pl.pallas_call(chain_kernel, out_shape=(jax.ShapeDtypeStruct((3, SLAB, HE...]
where the time goes in v3:
time: 73.3 us; the launch traced here: 73.1 us
  Pallas kernels  72.3 us (99%)
  between operations  0.8 us (1%)
    pallas_call x1, Pallas kernels, chain(): pl.pallas_call(chain_kernel, out_shape=(jax.ShapeDtypeStruct((3, SLAB, HE...  70 us
    pallas_call x1, Pallas kernels, settle(): pl.pallas_call(settle_kernel, out_shape=tuple((jax.ShapeDtypeStruct(a.sha...  2.34 us

profile of v3, /device:TPU:1, one launch (start us, length us, event | category | flops | bytes accessed | tf_op | source)
XLA Modules:
  0.0 73.1 jit_solution(8040909027970592297)
XLA Ops:
  0.6 70.0 %chain.1 = (f32[3,72,1024]{2,1,0:T(8,128)}, bf16[32,2304]{1,0:T(8,128)(2,1)}, f32[128,1024]{1,0:T(8,128)}) custom-call(s32[8]{0:T(128)} %doc_ref.1, bf16[128,2304]{1,0:T(8,128)(2,1)} %hid_ref.1, bf16[3,2304,1024]{2,1,0:T(8,128)(2,1)} %w_ref.1, f32[3,4,1024]{2,1,0:T(4,128)} %conv_ref.1, f32[128,1024]{1,0:T(8,128)} %ld_hbm.1, f32[8,128]{1,0:T(8,128)} %bitcast.3, ...), custom_call_target="tpu_custom_call" | custom-call | flops 8000000000 | bytes 18000000 | tf_op jit(solution)/shard_map/chain/pallas_call | solution.py:621
  70.6 2.3 %settle.1 = (f32[3,72,1024]{2,1,0:T(8,128)}, bf16[32,2304]{1,0:T(8,128)(2,1)}, f32[128,1024]{1,0:T(8,128)}) custom-call(f32[3,72,1024]{2,1,0:T(8,128)} %get-tuple-element.9.wg_ref, bf16[32,2304]{1,0:T(8,128)(2,1)} %get-tuple-element.10.ig_ref, f32[128,1024]{1,0:T(8,128)} %get-tuple-element.11.dld_ref), custom_call_target="tpu_custom_call" | custom-call | tf_op jit(solution)/shard_map/settle/pallas_call | solution.py:702

commit v4 on v3

--- a/solution.py
+++ b/solution.py
@@ -380,7 +380,7 @@
             block = jnp.concatenate([made[0][rows], made[1][rows]], axis=0)
             psend[unit, piece] = block.astype(BF16)
             part[unit, piece] = block
-        for step in range(1, ROWS):
+        for step in (2, 1, 3):
             part_copy(unit, step).start()
 
     def receive(unit):
@@ -392,15 +392,16 @@
         wg_ref[p, :, first : first + HALF] = total[:SLAB]
         wg_ref[p, :, first + HALF : first + 2 * HALF] = total[SLAB:]
 
-    def input_part(low, high):
+    def input_part(low, high, first, width):
+        cols = slice(first, first + width)
+
         def one(tile, carry):
             at = pl.ds(pl.multiple_of(tile * 256, 256), 256)
             total = jnp.zeros((TOK, 256), F32) if low == 0 else ipart[:, at]
             for p in range(low, high):
-                mine = own[p]
-                total = total + lax.dot_general(mine, wbuf[p, at, :], NT, preferred_element_type=F32)
+                total = total + lax.dot_general(own[p, :, cols], wbuf[p, at, cols], NT, preferred_element_type=F32)
             ipart[:, at] = total
-            if high == 3:
+            if first > 0:
                 isend[:, at] = total.astype(BF16)
             return carry
 
@@ -493,7 +494,7 @@
     share(1)
     finish(0)
     finish(1)
-    input_part(0, 1)
+    input_part(0, 1, 0, 1024)
 
     def returned(first, last):
         for j in range(first, last):
@@ -563,12 +564,13 @@
     spill_copy(1).wait_recv()
     set_out(2)
     set_out(3)
+    input_part(1, 3, 0, 512)
     spill_copy(2).wait_recv()
     set_out(4)
     set_out(5)
     hand_on(2)
     hand_on(3)
-    input_part(1, 3)
+    input_part(1, 3, 512, 512)
     for step in range(1, 4):
         input_copy(step).start()
     hand_on(4)

time: 73.3 us -> 71.4 us (0.974)
  Pallas kernels: 72.3 us -> 70.4 us
    pallas_call x1, Pallas kernels: 70 us -> 68.1 us  [chain(): pl.pallas_call(chain_kernel, out_shape=(jax.ShapeDtypeStruct((3, SLAB, HE...]
where the time goes in v4:
time: 71.4 us; the launch traced here: 71.2 us
  Pallas kernels  70.4 us (99%)
  between operations  0.8 us (1%)
    pallas_call x1, Pallas kernels, chain(): pl.pallas_call(chain_kernel, out_shape=(jax.ShapeDtypeStruct((3, SLAB, HE...  68.1 us
    pallas_call x1, Pallas kernels, settle(): pl.pallas_call(settle_kernel, out_shape=tuple((jax.ShapeDtypeStruct(a.sha...  2.34 us

profile of v4, /device:TPU:1, one launch (start us, length us, event | category | flops | bytes accessed | tf_op | source)
XLA Modules:
  0.0 71.2 jit_solution(911175384748216296)
XLA Ops:
  0.6 68.1 %chain.1 = (f32[3,72,1024]{2,1,0:T(8,128)}, bf16[32,2304]{1,0:T(8,128)(2,1)}, f32[128,1024]{1,0:T(8,128)}) custom-call(s32[8]{0:T(128)} %doc_ref.1, bf16[128,2304]{1,0:T(8,128)(2,1)} %hid_ref.1, bf16[3,2304,1024]{2,1,0:T(8,128)(2,1)} %w_ref.1, f32[3,4,1024]{2,1,0:T(4,128)} %conv_ref.1, f32[128,1024]{1,0:T(8,128)} %ld_hbm.1, f32[8,128]{1,0:T(8,128)} %bitcast.3, ...), custom_call_target="tpu_custom_call" | custom-call | flops 8000000000 | bytes 18000000 | tf_op jit(solution)/shard_map/chain/pallas_call | solution.py:623
  68.7 2.3 %settle.1 = (f32[3,72,1024]{2,1,0:T(8,128)}, bf16[32,2304]{1,0:T(8,128)(2,1)}, f32[128,1024]{1,0:T(8,128)}) custom-call(f32[3,72,1024]{2,1,0:T(8,128)} %get-tuple-element.9.wg_ref, bf16[32,2304]{1,0:T(8,128)(2,1)} %get-tuple-element.10.ig_ref, f32[128,1024]{1,0:T(8,128)} %get-tuple-element.11.dld_ref), custom_call_target="tpu_custom_call" | custom-call | tf_op jit(solution)/shard_map/settle/pallas_call | solution.py:704
